TPU v7x, 512 devices: a whole 4x4x16 slice. The times are simulated.
512 devices in a mesh: row: 16 (over x, y_hi, core), col: 32 (over z, y_lo).
Axes of the slice: x: 4, y: 4 (y_hi: 2, y_lo: 2; y = y_hi * 2 + y_lo), z: 16, core: 2. Of those that a mesh axis runs over, the one named last changes fastest.
Arguments:
- sigma: bfloat16 [2, 16384, 16384], P(None, 'row', 'col'), may hold values from -6 to 6
- coeffs: bfloat16 [2, 16384, 384], P(None, 'col'), may hold values from -0.046875 to 0.046875
Outputs:
- hamiltonian: bfloat16 [2, 16384, 16384], P(None, 'row', 'col')
- rotated: float32 [2, 384, 384], P(None, 'row', 'col')
All inputs are finite; a program needn't handle non-finite values.
Results may differ from a plain program's by a relative error of at most 0.0031.
Values may be sent and summed in bfloat16 or wider, within the bound.
No kernel may reach another device: no remote copies, remote signals or barrier semaphores. Data moves between devices by JAX's collectives and lax.ppermute only.
A program may use at most 64 MiB of HBM per device.

v0:
```python
import jax
import jax.numpy as jnp
from jax import lax
from jax.sharding import PartitionSpec as P


def spread(block, axis, source):
    block = jnp.where(lax.axis_index(axis) == source, block, jnp.zeros_like(block))
    return lax.psum(block, axis)


def move_columns(moving):
    return lax.all_to_all(moving, "col", split_axis=3, concat_axis=3, tiled=True)


def left_apply(left_panel, values):
    high = lax.Precision.HIGHEST
    part_re = jnp.dot(left_panel[0].T, values[0], precision=high) + jnp.dot(
        left_panel[1].T, values[1], precision=high
    )
    part_im = jnp.dot(left_panel[0].T, values[1], precision=high) - jnp.dot(
        left_panel[1].T, values[0], precision=high
    )
    return jnp.stack([part_re, part_im])


def body(sigma, coeffs):
    col_count = lax.axis_size("col")
    row_count = lax.axis_size("row")
    factor = col_count // row_count
    tile_height = sigma.shape[1]
    tile_width = sigma.shape[2]
    strip_rows = tile_width // col_count
    moving = sigma.reshape(2, 1, factor, col_count, strip_rows, tile_width)
    moving = move_columns(moving)
    moving = lax.all_to_all(moving, "row", split_axis=3, concat_axis=1, tiled=True)
    moving = move_columns(moving.reshape(2, 1, 1, col_count, factor, strip_rows, tile_width))
    mirror = moving.reshape(2, col_count, factor, strip_rows, tile_width)
    mirror = mirror.transpose(0, 2, 4, 1, 3).reshape(2, tile_height, tile_width).astype(jnp.float32)
    own_block = sigma.astype(jnp.float32)
    herm_re = 0.5 * (own_block[0] + mirror[0])
    herm_im = 0.5 * (own_block[1] - mirror[1])
    hamiltonian = jnp.stack([herm_re, herm_im]).astype(jnp.bfloat16)
    root_base = lax.axis_index("row") * factor
    panels = []
    for offset in range(factor):
        panels.append(spread(coeffs, "col", root_base + offset))
    left_panel = jnp.concatenate(panels, axis=1).astype(jnp.float32)
    prod_re = jnp.dot(hamiltonian[0], coeffs[0], preferred_element_type=jnp.float32) - jnp.dot(
        hamiltonian[1], coeffs[1], preferred_element_type=jnp.float32
    )
    prod_im = jnp.dot(hamiltonian[0], coeffs[1], preferred_element_type=jnp.float32) + jnp.dot(
        hamiltonian[1], coeffs[0], preferred_element_type=jnp.float32
    )
    product = jnp.stack([prod_re, prod_im])
    partial_value = lax.psum_scatter(
        left_apply(left_panel, product), "col", scatter_dimension=2, tiled=True
    )
    rotated = lax.psum_scatter(partial_value, "row", scatter_dimension=1, tiled=True)
    return (hamiltonian, rotated)


def solution(mesh):
    in_specs = (P(None, "row", "col"), P(None, "col", None))
    out_specs = (P(None, "row", "col"), P(None, "row", "col"))
    return jax.shard_map(body, mesh=mesh, in_specs=in_specs, out_specs=out_specs, check_vma=False)
```

profile of v0, /device:TPU:6, one launch (start us, length us, event | category | flops | bytes accessed | tf_op | source)
XLA Modules:
  0.0 831.7 jit_solution(3489439197454843713)
XLA Ops:
  7.2 1.8 copy.20
  9.0 115.0 %all_to_all.25 = bf16[2,1,2,32,16,512]{5,4,2,0,1,3:T(8,128)(2,1)S(1)} all-to-all(bf16[2,1,2,32,16,512]{5,4,2,0,1,3:T(8,128)(2,1)S(1)} %copy.20), channel_id=1, replica_groups=mesh['row'=16,'col'=32] {'col'}, dimensions={3} | all-to-all | bytes 4194304 | tf_op jit(solution)/shard_map/all_to_all | solution.py:13
  124.0 33.8 %all_to_all.26 = bf16[2,1,2,32,16,512]{5,4,2,0,1,3:T(8,128)(2,1)S(1)} all-to-all(bf16[2,1,2,32,16,512]{5,4,2,0,1,3:T(8,128)(2,1)S(1)} %all_to_all.25), channel_id=1, replica_groups=mesh['row'=16,'col'=32] {'row'}, dimensions={3} | all-to-all | bytes 4194304 | tf_op jit(solution)/shard_map/all_to_all | solution.py:36
  157.8 3.5 copy.21
  161.3 0.0 copy-start
  161.3 4.6 all-to-all-start.2
  165.9 0.0 all-reduce.8.cloned.1.call-start
  166.0 0.0 copy-done
  166.0 1.3 broadcast_select_fusion
  167.3 0.0 all-reduce.8.cloned.1.call-update
  167.3 0.0 all-reduce.6.cloned.1.call-start
  167.4 4.0 copy.19
  171.4 4.0 convert_element_type.15
  175.4 293.0 %all-reduce.8.cloned.1.call-done = (bf16[2,512,384]{2,1,0:T(8,128)(2,1)}, bf16[2,512,384]{2,1,0:T(8,128)(2,1)}) async-done(((bf16[2,512,384]{2,1,0:T(8,128)(2,1)}, bf16[2,512,384]{2,1,0:T(8,128)(2,1)}), (bf16[2,512,384]{2,1,0:T(8,128)(2,1)}, bf16[2,512,384]{2,1,0:T(8,128)(2,1)})) %all-reduce.8.cloned.1.call-update) | async-done | bytes 1572880 | tf_op jit(solution)/shard_map/psum | solution.py:9
  468.4 0.0 copy-start.1
  468.4 2.2 constant_dynamic-update-slice_fusion.1
  470.6 0.0 copy-done.1
  470.6 1.0 constant_dynamic-update-slice_fusion
  471.5 0.0 all-to-all-done.2
  471.5 1.7 convert_bitcast_fusion
  473.2 3.4 fusion.22
  476.6 4.0 slice.44
  480.7 2.8 slice.48
  483.4 4.6 fusion.3
  488.0 0.7 fusion.8
  488.8 0.7 fusion.10
  489.5 0.8 convolution_add_fusion
  490.3 0.7 convolution_subtract_fusion
  491.0 2.6 fusion.12
  493.6 2.6 fusion.13
  496.2 2.6 fusion.5
  498.8 2.6 fusion.4
  501.5 0.1 pad_maximum_fusion.1
  501.6 1.9 copy.22
  503.5 0.0 all-reduce.6.cloned.1.call-update
  503.5 1.3 dynamic-slice
  504.8 1.3 dynamic-slice.2
  507.3 1.5 pad_maximum_fusion
  508.9 3.9 copy.23
  512.8 254.7 %all-reduce.6.cloned.1.call-done = f32[2,384,384]{1,0,2:T(2,128)} async-done(((f32[2,384,384]{1,0,2:T(2,128)}), f32[2,384,384]{1,0,2:T(2,128)}) %all-reduce.6.cloned.1.call-update) | async-done | bytes 1179664
  767.5 0.8 constant_dynamic-slice_fusion.1
  768.3 55.8 %all-reduce.1 = f32[2,384,12]{1,0,2:T(2,128)S(1)} all-reduce(f32[2,384,12]{1,0,2:T(2,128)S(1)} %constant_dynamic-slice_fusion.1), channel_id=3, replica_groups=mesh['row'=16,'col'=32] {'row'}, use_global_device_ids=true, to_apply=%region_3.4.clone | all-reduce | flops 9216 | bytes 73728
  824.1 0.7 constant_dynamic-slice_fusion
Async XLA Ops:
  161.3 4.7 copy-start
  161.3 310.2 %all-to-all-start.2 = ((bf16[2,1,1,32,2,16,512]{6,4,5,0,2,1,3:T(2,128)(2,1)}), bf16[2,1,1,32,2,16,512]{6,4,5,0,2,1,3:T(2,128)(2,1)S(1)}, u32[]{:S(2)}, u32[]{:S(2)}) async-start(bf16[2,1,1,32,2,16,512]{6,4,5,0,2,1,3:T(2,128)(2,1)} %bitcast.57), calls=%async_computation.2 | async-start | bytes 4194304 | tf_op jit(solution)/shard_map/all_to_all | solution.py:13
  165.9 302.4 %all-reduce.8.cloned.1.call-start = ((), (), s32[]{:S(2)}) async-start(), calls=%async_computation.4 | async-start | bytes 3145728 | tf_op jit(solution)/shard_map/psum | solution.py:9
  167.3 600.2 %all-reduce.6.cloned.1.call-start = ((), (), s32[]{:S(2)}) async-start(), calls=%async_computation.3 | async-start | bytes 2359296
  468.4 2.2 copy-start.1
Sparse Core Ops, SparseCore 0:
  169.7 298.5 all-reduce.7
  503.6 263.8 all-reduce.5
where the time goes:
time: 841 us; the launch traced here: 832 us
  waiting for transfers between devices  548 us (65%)
  blocking collectives  205 us (24%)
  local copies, waits for them, and re-layouts  32.5 us (4%)
  between operations  15.5 us (2%)
  matrix products  13.4 us (2%)
  other arithmetic  13.2 us (2%)
    psum x1, waiting for transfers between devices, spread(): return lax.psum(block, axis)  293 us
    unnamed x3, waiting for transfers between devices  255 us
    all_to_all x1, blocking collectives, move_columns(): lax.all_to_all(moving, 'col', split_axis=3, concat_axis=3, tiled=True)  115 us
    unnamed x1, blocking collectives  55.8 us
    all_to_all x1, blocking collectives, body(): lax.all_to_all(moving, 'row', split_axis=3, concat_axis=1, tiled=True)  33.8 us
  transfers between devices with their start and end apart: 3, of which 2 were waited for; matrix products, arithmetic and copies ran while one was open for 2% of the time, Pallas kernels for 0%

commit v1 on v0

v1 whole, which is shorter than its diff:
```python
import jax
import jax.numpy as jnp
from jax import lax
from jax.experimental import pallas as pl
from jax.experimental.pallas import tpu as pltpu
from jax.sharding import PartitionSpec as P

BF16 = jnp.bfloat16
F32 = jnp.float32


def contract(left, right, dims):
    return lax.dot_general(left, right, (dims, ((), ())), preferred_element_type=F32)


def apply(left, right):
    return contract(left, right, ((1,), (0,)))


def apply_left_transposed(left, pieces):
    total = contract(left, pieces[0], ((0,), (0,)))
    for piece in pieces[1:]:
        total = total + contract(left, piece, ((0,), (0,)))
    return total


def split_exact(value):
    high = value.astype(BF16)
    rest = value - high.astype(F32)
    middle = rest.astype(BF16)
    low = (rest - middle.astype(F32)).astype(BF16)
    return high, middle, low


def rotate_kernel(which_ref, strip_ref, own_ref, other_ref, left_ref, out_ref):
    mine = which_ref[0]
    rows = strip_ref.shape[0] * strip_ref.shape[3]
    width = strip_ref.shape[4]

    def tile(side, part):
        return strip_ref[:, side, part].reshape(rows, width)

    own_re, own_im = tile(mine, 0), tile(mine, 1)
    prod_re = apply(own_re, own_ref[0]) - apply(own_im, own_ref[1])
    prod_im = apply(own_re, own_ref[1]) + apply(own_im, own_ref[0])
    far_re, far_im = tile(1 - mine, 0), tile(1 - mine, 1)
    prod_re += apply(far_re, other_ref[0]) - apply(far_im, other_ref[1])
    prod_im += apply(far_re, other_ref[1]) + apply(far_im, other_ref[0])
    states = left_ref.shape[3]
    left_re = left_ref[:, 0].reshape(rows, states)
    left_im = left_ref[:, 1].reshape(rows, states)
    pieces_re, pieces_im = split_exact(prod_re), split_exact(prod_im)
    rot_re = apply_left_transposed(left_re, pieces_re) + apply_left_transposed(left_im, pieces_im)
    rot_im = apply_left_transposed(left_re, pieces_im) - apply_left_transposed(left_im, pieces_re)
    out_ref[0] = 0.5 * (rot_re + rot_re.T)
    out_ref[1] = 0.5 * (rot_im - rot_im.T)


def rotate(which, strip, own, other, left):
    states = own.shape[2]
    vmem = pl.BlockSpec(memory_space=pltpu.VMEM)
    return pl.pallas_call(
        rotate_kernel,
        out_shape=jax.ShapeDtypeStruct((2, states, states), F32),
        in_specs=[pl.BlockSpec(memory_space=pltpu.SMEM), vmem, vmem, vmem, vmem],
        out_specs=vmem,
        compiler_params=pltpu.CompilerParams(vmem_limit_bytes=40 * 1024 * 1024),
        cost_estimate=pl.CostEstimate(flops=4 * 10**9, bytes_accessed=6 * 10**6, transcendentals=0),
    )(which, strip, own, other, left)


def hermitize_kernel(own_ref, mirror_ref, out_ref):
    size = own_ref.shape[2]
    mirror = mirror_ref[...].reshape(size, size).astype(F32).T
    own = own_ref[0].astype(F32)
    sign = jnp.where(pl.program_id(0) == 0, 1.0, -1.0).astype(F32)
    out_ref[0] = (0.5 * (own + sign * mirror)).astype(BF16)


def hermitize(sigma, mirror):
    _, height, width = sigma.shape
    strips, factor, _, strip_rows, _ = mirror.shape
    tile = pl.BlockSpec((1, width, width), lambda part, half: (part, half, 0))
    return pl.pallas_call(
        hermitize_kernel,
        grid=(2, factor),
        out_shape=jax.ShapeDtypeStruct(sigma.shape, BF16),
        in_specs=[
            tile,
            pl.BlockSpec((strips, 1, 1, strip_rows, width), lambda part, half: (0, half, part, 0, 0)),
        ],
        out_specs=tile,
        compiler_params=pltpu.CompilerParams(vmem_limit_bytes=32 * 1024 * 1024),
        cost_estimate=pl.CostEstimate(flops=4 * 10**6, bytes_accessed=6 * 10**6, transcendentals=0),
    )(sigma, mirror)


def exchange(value, dim, bit, axis, count, stride):
    partners = [(i, i ^ stride) for i in range(count)]
    kept = lax.dynamic_index_in_dim(value, bit, dim, keepdims=False)
    given = lax.dynamic_index_in_dim(value, 1 - bit, dim, keepdims=False)
    return kept, lax.ppermute(given, axis, partners)


def halve(value, dim, bit, axis, count, stride):
    kept, got = exchange(value, dim, bit, axis, count, stride)
    return kept + got


def body(sigma, coeffs):
    row_count = lax.axis_size("row")
    col_count = lax.axis_size("col")
    states = coeffs.shape[2]
    factor = col_count // row_count
    depth = col_count // factor
    _, tile_height, tile_width = sigma.shape
    strip_rows = tile_width // row_count
    row = lax.axis_index("row")
    col = lax.axis_index("col")
    side = col % factor

    plane = [
        [r * col_count + factor * z + low for r in range(row_count) for low in range(factor)]
        for z in range(depth)
    ]
    along_z = [[factor * z + low for z in range(depth)] for low in range(factor)]
    swap = [(c, c ^ 1) for c in range(col_count)]

    own_rows = lax.dynamic_slice_in_dim(coeffs, row * strip_rows, strip_rows, 1)
    left = lax.all_gather(own_rows, "col", axis=0, tiled=True, axis_index_groups=along_z)
    left = left.reshape(depth, 2, strip_rows, states)
    other = lax.ppermute(coeffs, "col", swap)

    moving = sigma.reshape(2, factor, row_count, strip_rows, tile_width).transpose(2, 1, 0, 3, 4)
    moving = moving.reshape(row_count * factor, 2, strip_rows, tile_width)
    moving = lax.all_to_all(moving, ("row", "col"), 0, 0, tiled=True, axis_index_groups=plane)
    moving, left = lax.optimization_barrier((moving, left))
    strip = moving.reshape(row_count, factor, 2, strip_rows, tile_width)

    moving = lax.all_to_all(strip, "col", 0, 0, tiled=True, axis_index_groups=along_z)

    term = rotate(side.astype(jnp.int32).reshape(1), strip, coeffs, other, left)
    rest = states // row_count
    core = row % 2
    bits = (row // 8, (row // 4) % 2, (row // 2) % 2)
    part_sum = halve(term.reshape(2, row_count // 2, 2, rest, states), 2, core, "row", row_count, 1)
    part_sum = halve(part_sum, 0, side, "col", col_count, 1)
    part_sum = part_sum.reshape(2, row_count // 4, rest, states)
    part_sum = halve(part_sum, 0, bits[0], "row", row_count, 8)
    part_sum = part_sum.reshape(2, row_count // 8, rest, states)
    part_sum = halve(part_sum, 0, bits[1], "row", row_count, 4)
    part_sum = halve(part_sum, 0, bits[2], "row", row_count, 2)
    part_sum = part_sum.T
    level = depth // 2
    while level:
        part_sum = part_sum.reshape(2, part_sum.shape[0] // 2, rest)
        part_sum = halve(part_sum, 0, (col // (factor * level)) % 2, "col", col_count, factor * level)
        if level == depth // 2:
            moving, part_sum = lax.optimization_barrier((moving, part_sum))
        level //= 2
    part_sum = part_sum.reshape(factor, states // col_count, rest)
    mine, got = exchange(part_sum, 0, side, "col", col_count, 1)
    real = jnp.where(side == 0, mine, got)
    imag = jnp.where(side == 0, got, mine)
    rotated = jnp.stack([real.T, imag.T])

    mirror = lax.all_to_all(moving, "row", 0, 0, tiled=True)
    hamiltonian = hermitize(sigma, mirror)
    return (hamiltonian, rotated)


def solution(mesh):
    in_specs = (P(None, "row", "col"), P(None, "col", None))
    out_specs = (P(None, "row", "col"), P(None, "row", "col"))
    return jax.shard_map(body, mesh=mesh, in_specs=in_specs, out_specs=out_specs, check_vma=False)
```

time: 841 us -> 198 us (0.24)
  waiting for transfers between devices: 548 us -> 78.5 us
  blocking collectives: 205 us -> 37.5 us
  starting transfers between devices: 4.67 us -> 63.6 us
  local copies, waits for them, and re-layouts: 32.5 us -> 4.55 us
  between operations: 15.5 us -> 1.16 us
  matrix products: 13.4 us -> 0 us
  other arithmetic: 13.2 us -> 0.16 us
  Pallas kernels: 0 us -> 10.8 us
    psum x1 -> x0, waiting for transfers between devices: 293 us -> none  [spread(): return lax.psum(block, axis)]
    unnamed x3 -> x0, waiting for transfers between devices: 255 us -> none
    all_to_all x2 -> x0, blocking collectives: 149 us -> none  [the longest x1 115 us: move_columns(): lax.all_to_all(moving, 'col', split_axis=3, concat_axis=3, tiled=True)]
    ppermute x0 -> x11, waiting for transfers between devices: none -> 78.5 us  [the longest x10 63.7 us: exchange(): return (kept, lax.ppermute(given, axis, partners))]
    unnamed x1 -> x0, blocking collectives: 55.8 us -> none
    ppermute x0 -> x11, starting transfers between devices: none -> 40.5 us  [the longest x10 37.2 us: exchange(): return (kept, lax.ppermute(given, axis, partners))]
    all_gather x0 -> x1, blocking collectives: none -> 37.5 us  [body(): lax.all_gather(own_rows, 'col', axis=0, tiled=True, axis_index_groups=alo...]
    all_to_all x1 -> x3, starting transfers between devices: 4.59 us -> 23.1 us  [the longest x1 10.5 us: body(): lax.all_to_all(moving, ('row', 'col'), 0, 0, tiled=True, axis_index_group...]
  transfers between devices with their start and end apart: 3 -> 14, of which waited for: 2 -> 11; matrix products, arithmetic and copies ran while one was open for 2% -> 1% of each run, Pallas kernels for 0% -> 3%
where the time goes in v1:
time: 198 us; the launch traced here: 196 us
  waiting for transfers between devices  78.5 us (40%)
  starting transfers between devices  63.6 us (32%)
  blocking collectives  37.5 us (19%)
  Pallas kernels  10.8 us (5%)
  local copies, waits for them, and re-layouts  4.55 us (2%)
    ppermute x10, waiting for transfers between devices, exchange(): return (kept, lax.ppermute(given, axis, partners))  63.7 us
    all_gather x1, blocking collectives, body(): lax.all_gather(own_rows, 'col', axis=0, tiled=True, axis_index_groups=alo...  37.5 us
    ppermute x10, starting transfers between devices, exchange(): return (kept, lax.ppermute(given, axis, partners))  37.2 us
    ppermute x1, waiting for transfers between devices, body(): other = lax.ppermute(coeffs, 'col', swap)  14.8 us
    all_to_all x1, starting transfers between devices, body(): lax.all_to_all(moving, ('row', 'col'), 0, 0, tiled=True, axis_index_group...  10.5 us
    pallas_call x1, Pallas kernels, rotate(): pl.pallas_call(rotate_kernel, out_shape=jax.ShapeDtypeStruct((2, states,...  6.53 us
    all_to_all x1, starting transfers between devices, body(): lax.all_to_all(strip, 'col', 0, 0, tiled=True, axis_index_groups=along_z)  6.32 us
    all_to_all x1, starting transfers between devices, body(): mirror = lax.all_to_all(moving, 'row', 0, 0, tiled=True)  6.29 us
  transfers between devices with their start and end apart: 14, of which 11 were waited for; matrix products, arithmetic and copies ran while one was open for 1% of the time, Pallas kernels for 3%

profile of v1, /device:TPU:6, one launch (start us, length us, event | category | flops | bytes accessed | tf_op | source)
XLA Modules:
  0.0 196.3 jit_solution(123497535784790727)
XLA Ops:
  0.6 3.2 %copy.16 = bf16[16,2,2,32,512]{4,3,2,1,0:T(8,128)(2,1)} copy(bf16[16,2,2,32,512]{4,3,0,1,2:T(8,128)(2,1)} %bitcast.71) | data formatting | bytes 4194304 | tf_op jit(solution)/shard_map/transpose | solution.py:134
  3.8 0.0 copy-start.1
  3.8 10.5 %all-to-all-start = ((bf16[32,2,32,512]{3,2,1,0:T(8,128)(2,1)}), bf16[32,2,32,512]{3,2,1,0:T(8,128)(2,1)}, u32[]{:S(2)}, u32[]{:S(2)}) async-start(bf16[32,2,32,512]{3,2,1,0:T(8,128)(2,1)} %bitcast.2), calls=%async_computation | async-start | bytes 4194304 | tf_op jit(solution)/shard_map/all_to_all | solution.py:136
  14.3 0.0 copy-done.1
  14.3 37.5 %all_gather.3 = bf16[32,32,384]{2,1,0:T(8,128)(2,1)S(1)} all-gather(bf16[2,32,384]{2,1,0:T(8,128)(2,1)S(1)} %constant_dynamic-slice_fusion.8), channel_id=1, replica_groups={{0,2,4,6,8,10,12,14,16,18,20,22,24,26,28,30},{1,3,5,7,9,11,13,15,17,19,..., dimensions={0}, use_global_device_ids=true | all-gather | bytes 835584 | tf_op jit(solution)/shard_map/all_gather | solution.py:130
  51.8 0.0 all-to-all-done
  51.8 6.3 %all-to-all-start.1 = ((bf16[16,2,2,32,512]{4,3,2,1,0:T(8,128)(2,1)}), bf16[16,2,2,32,512]{4,3,2,1,0:T(8,128)(2,1)}, u32[]{:S(2)}, u32[]{:S(2)}) async-start(bf16[16,2,2,32,512]{4,3,2,1,0:T(8,128)(2,1)} %bitcast.4.strip_ref), calls=%async_computation.1 | async-start | bytes 4194304 | tf_op jit(solution)/shard_map/all_to_all | solution.py:140
  58.1 3.4 %collective-permute-start = (bf16[2,512,384]{2,1,0:T(8,128)(2,1)S(1)}, bf16[2,512,384]{2,1,0:T(8,128)(2,1)S(1)}, u32[]{:S(2)}, u32[]{:S(2)}) collective-permute-start(bf16[2,512,384]{2,1,0:T(8,128)(2,1)S(1)} %copy-done.1), channel_id=1, source_target_pairs={{0,1},{1,0},{2,3},{3,2},{4,5},{5,4},{6,7},{7,6},{8,9},{9,8},{10,11... | collective-permute-start | bytes 2359304 | tf_op jit(solution)/shard_map/ppermute | solution.py:132
  61.6 14.8 %collective-permute-done.other_ref = bf16[2,512,384]{2,1,0:T(8,128)(2,1)S(1)} collective-permute-done((bf16[2,512,384]{2,1,0:T(8,128)(2,1)S(1)}, bf16[2,512,384]{2,1,0:T(8,128)(2,1)S(1)}, u32[]{:S(2)}, u32[]{:S(2)}) %collective-permute-start) | collective-permute-done | bytes 786464 | tf_op jit(solution)/shard_map/ppermute | solution.py:132
  76.3 6.5 %shard_map.41 = f32[2,384,384]{2,1,0:T(8,128)S(1)} custom-call(s32[1]{0:T(128)} %bitcast.5.which_ref, bf16[16,2,2,32,512]{4,3,2,1,0:T(8,128)(2,1)} %bitcast.4.strip_ref, bf16[2,512,384]{2,1,0:T(8,128)(2,1)S(1)} %copy-done.1, bf16[2,512,384]{2,1,0:T(8,128)(2,1)S(1)} %collective-permute-done.other_ref, bf16[16,2,32,384]{3,2,1,0:T(8,128)(2,1)S(1)} %bitcast.74), custom_call_target="tpu_custom_call" | custom-call | flops 4000000000 | bytes 6000000 | tf_op jit(solution)/shard_map/pallas_call | solution.py:62
  82.9 1.9 collective-permute-start.1
  84.9 2.0 collective-permute-done.1
  86.8 0.1 bitcast_add_fusion
  86.9 2.7 %collective-permute-start.2 = (f32[8,24,384]{2,1,0:T(8,128)S(1)}, f32[8,24,384]{2,1,0:T(8,128)S(1)}, u32[]{:S(2)}, u32[]{:S(2)}) collective-permute-start(f32[8,24,384]{2,1,0:T(8,128)S(1)} %dynamic-slice_bitcast_fusion.1), channel_id=1, source_target_pairs={{0,1},{1,0},{2,3},{3,2},{4,5},{5,4},{6,7},{7,6},{8,9},{9,8},{10,11... | collective-permute-start | bytes 884744 | tf_op jit(solution)/shard_map/ppermute | solution.py:102
  89.6 8.3 %collective-permute-done.2 = f32[8,24,384]{2,1,0:T(8,128)S(1)} collective-permute-done((f32[8,24,384]{2,1,0:T(8,128)S(1)}, f32[8,24,384]{2,1,0:T(8,128)S(1)}, u32[]{:S(2)}, u32[]{:S(2)}) %collective-permute-start.2) | collective-permute-done | bytes 294944 | tf_op jit(solution)/shard_map/ppermute | solution.py:102
  97.9 3.4 %collective-permute-start.3 = (f32[4,24,384]{2,1,0:T(8,128)S(1)}, f32[4,24,384]{2,1,0:T(8,128)S(1)}, u32[]{:S(2)}, u32[]{:S(2)}) collective-permute-start(f32[4,24,384]{2,1,0:T(8,128)S(1)} %dynamic-slice_bitcast_fusion.2), channel_id=1, source_target_pairs={{0,256},{32,288},{64,320},{96,352},{128,384},{160,416},{192,448},{... | collective-permute-start | bytes 442376 | tf_op jit(solution)/shard_map/ppermute | solution.py:102
  101.4 5.1 %collective-permute-done.3 = f32[4,24,384]{2,1,0:T(8,128)S(1)} collective-permute-done((f32[4,24,384]{2,1,0:T(8,128)S(1)}, f32[4,24,384]{2,1,0:T(8,128)S(1)}, u32[]{:S(2)}, u32[]{:S(2)}) %collective-permute-start.3) | collective-permute-done | bytes 147488 | tf_op jit(solution)/shard_map/ppermute | solution.py:102
  106.6 2.2 %collective-permute-start.4 = (f32[2,24,384]{2,1,0:T(8,128)S(1)}, f32[2,24,384]{2,1,0:T(8,128)S(1)}, u32[]{:S(2)}, u32[]{:S(2)}) collective-permute-start(f32[2,24,384]{2,1,0:T(8,128)S(1)} %dynamic-slice_bitcast_fusion.3), channel_id=1, source_target_pairs={{0,128},{32,160},{64,192},{96,224},{128,0},{160,32},{192,64},{224,... | collective-permute-start | bytes 221192 | tf_op jit(solution)/shard_map/ppermute | solution.py:102
  108.8 4.0 %collective-permute-done.4 = f32[2,24,384]{2,1,0:T(8,128)S(1)} collective-permute-done((f32[2,24,384]{2,1,0:T(8,128)S(1)}, f32[2,24,384]{2,1,0:T(8,128)S(1)}, u32[]{:S(2)}, u32[]{:S(2)}) %collective-permute-start.4) | collective-permute-done | bytes 73760 | tf_op jit(solution)/shard_map/ppermute | solution.py:102
  112.8 3.9 %collective-permute-start.5 = (f32[24,384]{1,0:T(8,128)S(1)}, f32[24,384]{1,0:T(8,128)S(1)}, u32[]{:S(2)}, u32[]{:S(2)}) collective-permute-start(f32[24,384]{1,0:T(8,128)S(1)} %dynamic-slice_bitcast_fusion.4), channel_id=1, source_target_pairs={{0,64},{32,96},{64,0},{96,32},{128,192},{160,224},{192,128},{224,1... | collective-permute-start | bytes 110600 | tf_op jit(solution)/shard_map/ppermute | solution.py:102
  116.8 3.4 %collective-permute-done.5 = f32[24,384]{1,0:T(8,128)S(1)} collective-permute-done((f32[24,384]{1,0:T(8,128)S(1)}, f32[24,384]{1,0:T(8,128)S(1)}, u32[]{:S(2)}, u32[]{:S(2)}) %collective-permute-start.5) | collective-permute-done | bytes 36896 | tf_op jit(solution)/shard_map/ppermute | solution.py:102
  120.2 0.1 reshape.51
  120.4 12.2 %collective-permute-start.6 = (f32[192,24]{0,1:T(8,128)S(1)}, f32[192,24]{0,1:T(8,128)S(1)}, u32[]{:S(2)}, u32[]{:S(2)}) collective-permute-start(f32[192,24]{0,1:T(8,128)S(1)} %bitcast.81), channel_id=1, source_target_pairs={{0,16},{1,17},{2,18},{3,19},{4,20},{5,21},{6,22},{7,23},{8,24},{9,... | collective-permute-start | bytes 55304 | tf_op jit(solution)/shard_map/ppermute | solution.py:102
  132.6 24.9 %collective-permute-done.6 = f32[192,24]{0,1:T(8,128)S(1)} collective-permute-done((f32[192,24]{0,1:T(8,128)S(1)}, f32[192,24]{0,1:T(8,128)S(1)}, u32[]{:S(2)}, u32[]{:S(2)}) %collective-permute-start.6) | collective-permute-done | bytes 18464 | tf_op jit(solution)/shard_map/ppermute | solution.py:102
  157.6 0.0 copy-start
  157.6 0.0 all-to-all-done.1
  157.6 6.3 %all-to-all-start.2 = ((bf16[16,2,2,32,512]{4,3,2,1,0:T(8,128)(2,1)}), bf16[16,2,2,32,512]{4,3,2,1,0:T(8,128)(2,1)}, u32[]{:S(2)}, u32[]{:S(2)}) async-start(bf16[16,2,2,32,512]{4,3,2,1,0:T(8,128)(2,1)} %all-to-all-done.1), calls=%async_computation.2 | async-start | bytes 4194304 | tf_op jit(solution)/shard_map/all_to_all | solution.py:167
  163.9 0.1 reshape.52
  164.0 1.9 collective-permute-start.7
  165.9 7.5 %collective-permute-done.7 = f32[96,24]{0,1:T(8,128)S(1)} collective-permute-done((f32[96,24]{0,1:T(8,128)S(1)}, f32[96,24]{0,1:T(8,128)S(1)}, u32[]{:S(2)}, u32[]{:S(2)}) %collective-permute-start.7) | collective-permute-done | bytes 9248 | tf_op jit(solution)/shard_map/ppermute | solution.py:102
  173.5 0.1 reshape.53
  173.6 2.8 %collective-permute-start.8 = (f32[48,24]{0,1:T(8,128)S(1)}, f32[48,24]{0,1:T(8,128)S(1)}, u32[]{:S(2)}, u32[]{:S(2)}) collective-permute-start(f32[48,24]{0,1:T(8,128)S(1)} %bitcast.84), channel_id=1, source_target_pairs={{0,4},{1,5},{2,6},{3,7},{4,0},{5,1},{6,2},{7,3},{8,12},{9,13},{10,... | collective-permute-start | bytes 13832 | tf_op jit(solution)/shard_map/ppermute | solution.py:102
  176.4 3.7 %collective-permute-done.8 = f32[48,24]{0,1:T(8,128)S(1)} collective-permute-done((f32[48,24]{0,1:T(8,128)S(1)}, f32[48,24]{0,1:T(8,128)S(1)}, u32[]{:S(2)}, u32[]{:S(2)}) %collective-permute-start.8) | collective-permute-done | bytes 4640 | tf_op jit(solution)/shard_map/ppermute | solution.py:102
  180.1 0.1 reshape.54
  180.2 0.1 copy.18
  180.3 3.5 %collective-permute-start.9 = (f32[24,24]{1,0:T(8,128)S(1)}, f32[24,24]{1,0:T(8,128)S(1)}, u32[]{:S(2)}, u32[]{:S(2)}) collective-permute-start(f32[24,24]{1,0:T(8,128)S(1)} %bitcast.82), channel_id=1, source_target_pairs={{0,2},{1,3},{2,0},{3,1},{4,6},{5,7},{6,4},{7,5},{8,10},{9,11},{10,... | collective-permute-start | bytes 6920 | tf_op jit(solution)/shard_map/ppermute | solution.py:102
  183.8 0.1 copy.17
  183.8 2.0 %collective-permute-done.9 = f32[24,24]{1,0:T(8,128)S(1)} collective-permute-done((f32[24,24]{1,0:T(8,128)S(1)}, f32[24,24]{1,0:T(8,128)S(1)}, u32[]{:S(2)}, u32[]{:S(2)}) %collective-permute-start.9) | collective-permute-done | bytes 2336 | tf_op jit(solution)/shard_map/ppermute | solution.py:102
  185.9 2.7 %collective-permute-start.10 = (f32[12,24]{1,0:T(8,128)S(1)}, f32[12,24]{1,0:T(8,128)S(1)}, u32[]{:S(2)}, u32[]{:S(2)}) collective-permute-start(f32[12,24]{1,0:T(8,128)S(1)} %dynamic-slice_bitcast_fusion.5), channel_id=1, source_target_pairs={{0,1},{1,0},{2,3},{3,2},{4,5},{5,4},{6,7},{7,6},{8,9},{9,8},{10,11... | collective-permute-start | bytes 3464 | tf_op jit(solution)/shard_map/ppermute | solution.py:102
  188.6 2.8 %collective-permute-done.10 = f32[12,24]{1,0:T(8,128)S(1)} collective-permute-done((f32[12,24]{1,0:T(8,128)S(1)}, f32[12,24]{1,0:T(8,128)S(1)}, u32[]{:S(2)}, u32[]{:S(2)}) %collective-permute-start.10) | collective-permute-done | bytes 1184 | tf_op jit(solution)/shard_map/ppermute | solution.py:102
  191.4 0.6 copy.19
  192.0 0.0 all-to-all-done.2.mirror_ref
  192.1 0.0 copy-done
  192.1 4.3 %shard_map.42 = bf16[2,1024,512]{2,1,0:T(8,128)(2,1)} custom-call(bf16[2,1024,512]{2,1,0:T(8,128)(2,1)S(1)} %copy-done, bf16[16,2,2,32,512]{4,3,2,1,0:T(8,128)(2,1)} %all-to-all-done.2.mirror_ref), custom_call_target="tpu_custom_call" | custom-call | flops 4000000 | bytes 6000000 | tf_op jit(solution)/shard_map/pallas_call | solution.py:84
  (23 shorter events, 0.4 us)
Async XLA Ops:
  3.8 10.5 %copy-start.1 = (bf16[2,512,384]{2,1,0:T(8,128)(2,1)S(1)}, bf16[2,512,384]{2,1,0:T(8,128)(2,1)}, u32[]{:S(2)}) copy-start(bf16[2,512,384]{2,1,0:T(8,128)(2,1)} %own_ref.2) | copy-start | bytes 2359300
  3.8 48.0 %all-to-all-start = ((bf16[32,2,32,512]{3,2,1,0:T(8,128)(2,1)}), bf16[32,2,32,512]{3,2,1,0:T(8,128)(2,1)}, u32[]{:S(2)}, u32[]{:S(2)}) async-start(bf16[32,2,32,512]{3,2,1,0:T(8,128)(2,1)} %bitcast.2), calls=%async_computation | async-start | bytes 4194304 | tf_op jit(solution)/shard_map/all_to_all | solution.py:136
  51.8 105.7 %all-to-all-start.1 = ((bf16[16,2,2,32,512]{4,3,2,1,0:T(8,128)(2,1)}), bf16[16,2,2,32,512]{4,3,2,1,0:T(8,128)(2,1)}, u32[]{:S(2)}, u32[]{:S(2)}) async-start(bf16[16,2,2,32,512]{4,3,2,1,0:T(8,128)(2,1)} %bitcast.4.strip_ref), calls=%async_computation.1 | async-start | bytes 4194304 | tf_op jit(solution)/shard_map/all_to_all | solution.py:140
  58.1 18.2 %collective-permute-start = (bf16[2,512,384]{2,1,0:T(8,128)(2,1)S(1)}, bf16[2,512,384]{2,1,0:T(8,128)(2,1)S(1)}, u32[]{:S(2)}, u32[]{:S(2)}) collective-permute-start(bf16[2,512,384]{2,1,0:T(8,128)(2,1)S(1)} %copy-done.1), channel_id=1, source_target_pairs={{0,1},{1,0},{2,3},{3,2},{4,5},{5,4},{6,7},{7,6},{8,9},{9,8},{10,11... | collective-permute-start | bytes 2359304 | tf_op jit(solution)/shard_map/ppermute | solution.py:132
  82.9 3.9 %collective-permute-start.1 = (f32[2,8,24,384]{3,2,1,0:T(8,128)S(1)}, f32[2,8,24,384]{3,2,1,0:T(8,128)S(1)}, u32[]{:S(2)}, u32[]{:S(2)}) collective-permute-start(f32[2,8,24,384]{3,2,1,0:T(8,128)S(1)} %dynamic-slice_bitcast_fusion), channel_id=1, source_target_pairs={{0,32},{32,0},{64,96},{96,64},{128,160},{160,128},{192,224},{224,1... | collective-permute-start | bytes 1769480 | tf_op jit(solution)/shard_map/ppermute | solution.py:102
  86.9 11.0 %collective-permute-start.2 = (f32[8,24,384]{2,1,0:T(8,128)S(1)}, f32[8,24,384]{2,1,0:T(8,128)S(1)}, u32[]{:S(2)}, u32[]{:S(2)}) collective-permute-start(f32[8,24,384]{2,1,0:T(8,128)S(1)} %dynamic-slice_bitcast_fusion.1), channel_id=1, source_target_pairs={{0,1},{1,0},{2,3},{3,2},{4,5},{5,4},{6,7},{7,6},{8,9},{9,8},{10,11... | collective-permute-start | bytes 884744 | tf_op jit(solution)/shard_map/ppermute | solution.py:102
  97.9 8.6 %collective-permute-start.3 = (f32[4,24,384]{2,1,0:T(8,128)S(1)}, f32[4,24,384]{2,1,0:T(8,128)S(1)}, u32[]{:S(2)}, u32[]{:S(2)}) collective-permute-start(f32[4,24,384]{2,1,0:T(8,128)S(1)} %dynamic-slice_bitcast_fusion.2), channel_id=1, source_target_pairs={{0,256},{32,288},{64,320},{96,352},{128,384},{160,416},{192,448},{... | collective-permute-start | bytes 442376 | tf_op jit(solution)/shard_map/ppermute | solution.py:102
  106.6 6.2 %collective-permute-start.4 = (f32[2,24,384]{2,1,0:T(8,128)S(1)}, f32[2,24,384]{2,1,0:T(8,128)S(1)}, u32[]{:S(2)}, u32[]{:S(2)}) collective-permute-start(f32[2,24,384]{2,1,0:T(8,128)S(1)} %dynamic-slice_bitcast_fusion.3), channel_id=1, source_target_pairs={{0,128},{32,160},{64,192},{96,224},{128,0},{160,32},{192,64},{224,... | collective-permute-start | bytes 221192 | tf_op jit(solution)/shard_map/ppermute | solution.py:102
  112.8 7.4 %collective-permute-start.5 = (f32[24,384]{1,0:T(8,128)S(1)}, f32[24,384]{1,0:T(8,128)S(1)}, u32[]{:S(2)}, u32[]{:S(2)}) collective-permute-start(f32[24,384]{1,0:T(8,128)S(1)} %dynamic-slice_bitcast_fusion.4), channel_id=1, source_target_pairs={{0,64},{32,96},{64,0},{96,32},{128,192},{160,224},{192,128},{224,1... | collective-permute-start | bytes 110600 | tf_op jit(solution)/shard_map/ppermute | solution.py:102
  120.4 37.2 %collective-permute-start.6 = (f32[192,24]{0,1:T(8,128)S(1)}, f32[192,24]{0,1:T(8,128)S(1)}, u32[]{:S(2)}, u32[]{:S(2)}) collective-permute-start(f32[192,24]{0,1:T(8,128)S(1)} %bitcast.81), channel_id=1, source_target_pairs={{0,16},{1,17},{2,18},{3,19},{4,20},{5,21},{6,22},{7,23},{8,24},{9,... | collective-permute-start | bytes 55304 | tf_op jit(solution)/shard_map/ppermute | solution.py:102
  157.6 34.5 %copy-start = (bf16[2,1024,512]{2,1,0:T(8,128)(2,1)S(1)}, bf16[2,1024,512]{2,1,0:T(8,128)(2,1)}, u32[]{:S(2)}) copy-start(bf16[2,1024,512]{2,1,0:T(8,128)(2,1)} %own_ref.3) | copy-start | bytes 6291460
  157.6 34.5 %all-to-all-start.2 = ((bf16[16,2,2,32,512]{4,3,2,1,0:T(8,128)(2,1)}), bf16[16,2,2,32,512]{4,3,2,1,0:T(8,128)(2,1)}, u32[]{:S(2)}, u32[]{:S(2)}) async-start(bf16[16,2,2,32,512]{4,3,2,1,0:T(8,128)(2,1)} %all-to-all-done.1), calls=%async_computation.2 | async-start | bytes 4194304 | tf_op jit(solution)/shard_map/all_to_all | solution.py:167
  164.0 9.5 %collective-permute-start.7 = (f32[96,24]{0,1:T(8,128)S(1)}, f32[96,24]{0,1:T(8,128)S(1)}, u32[]{:S(2)}, u32[]{:S(2)}) collective-permute-start(f32[96,24]{0,1:T(8,128)S(1)} %bitcast.83), channel_id=1, source_target_pairs={{0,8},{1,9},{2,10},{3,11},{4,12},{5,13},{6,14},{7,15},{8,0},{9,1},... | collective-permute-start | bytes 27656 | tf_op jit(solution)/shard_map/ppermute | solution.py:102
  173.6 6.5 %collective-permute-start.8 = (f32[48,24]{0,1:T(8,128)S(1)}, f32[48,24]{0,1:T(8,128)S(1)}, u32[]{:S(2)}, u32[]{:S(2)}) collective-permute-start(f32[48,24]{0,1:T(8,128)S(1)} %bitcast.84), channel_id=1, source_target_pairs={{0,4},{1,5},{2,6},{3,7},{4,0},{5,1},{6,2},{7,3},{8,12},{9,13},{10,... | collective-permute-start | bytes 13832 | tf_op jit(solution)/shard_map/ppermute | solution.py:102
  180.3 5.6 %collective-permute-start.9 = (f32[24,24]{1,0:T(8,128)S(1)}, f32[24,24]{1,0:T(8,128)S(1)}, u32[]{:S(2)}, u32[]{:S(2)}) collective-permute-start(f32[24,24]{1,0:T(8,128)S(1)} %bitcast.82), channel_id=1, source_target_pairs={{0,2},{1,3},{2,0},{3,1},{4,6},{5,7},{6,4},{7,5},{8,10},{9,11},{10,... | collective-permute-start | bytes 6920 | tf_op jit(solution)/shard_map/ppermute | solution.py:102
  185.9 5.5 %collective-permute-start.10 = (f32[12,24]{1,0:T(8,128)S(1)}, f32[12,24]{1,0:T(8,128)S(1)}, u32[]{:S(2)}, u32[]{:S(2)}) collective-permute-start(f32[12,24]{1,0:T(8,128)S(1)} %dynamic-slice_bitcast_fusion.5), channel_id=1, source_target_pairs={{0,1},{1,0},{2,3},{3,2},{4,5},{5,4},{6,7},{7,6},{8,9},{9,8},{10,11... | collective-permute-start | bytes 3464 | tf_op jit(solution)/shard_map/ppermute | solution.py:102

commit v2 on v0

v2 whole, which is shorter than its diff:
```python
import jax
import jax.numpy as jnp
from jax import lax
from jax.experimental import pallas as pl
from jax.experimental.pallas import tpu as pltpu
from jax.sharding import PartitionSpec as P

BF16 = jnp.bfloat16
F32 = jnp.float32
ORDER = (0, 4, 2, 6, 1, 5, 3, 7)
STRIDE = 5


def contract(left, right, dims):
    return lax.dot_general(left, right, (dims, ((), ())), preferred_element_type=F32)


def apply(left, right):
    return contract(left, right, ((1,), (0,)))


def split_exact(value):
    high = value.astype(BF16)
    rest = value - high.astype(F32)
    middle = rest.astype(BF16)
    low = (rest - middle.astype(F32)).astype(BF16)
    return high, middle, low


def multiply(strip_ref, side, block_ref):
    rows = strip_ref.shape[0] * strip_ref.shape[3]
    width = strip_ref.shape[4]
    real = strip_ref[:, side, 0].reshape(rows, width)
    imag = strip_ref[:, side, 1].reshape(rows, width)
    prod_re = apply(real, block_ref[0]) - apply(imag, block_ref[1])
    prod_im = apply(real, block_ref[1]) + apply(imag, block_ref[0])
    return prod_re, prod_im


def near_kernel(which_ref, strip_ref, own_ref, out_ref):
    out_ref[0], out_ref[1] = multiply(strip_ref, which_ref[0], own_ref)


def rotate_kernel(which_ref, strip_ref, near_ref, other_ref, left_ref, out_ref):
    prod_re, prod_im = multiply(strip_ref, 1 - which_ref[0], other_ref)
    prod_re += near_ref[0]
    prod_im += near_ref[1]
    rows = near_ref.shape[1]
    states = left_ref.shape[3]
    left = jnp.concatenate(
        [left_ref[:, 0].reshape(rows, states).T, left_ref[:, 1].reshape(rows, states).T], axis=1
    )
    rot_re = rot_im = None
    for real, imag in zip(split_exact(prod_re), split_exact(prod_im)):
        add_re = apply(left, jnp.concatenate([real, imag], axis=0))
        add_im = apply(left, jnp.concatenate([imag, -real], axis=0))
        rot_re = add_re if rot_re is None else rot_re + add_re
        rot_im = add_im if rot_im is None else rot_im + add_im
    rot_re = 0.5 * (rot_re + rot_re.T)
    rot_im = 0.5 * (rot_im - rot_im.T)
    blocks, _, height, _ = out_ref.shape
    for block in range(blocks):
        out_ref[block, 0] = rot_re[block * height : (block + 1) * height]
        out_ref[block, 1] = rot_im[block * height : (block + 1) * height]


def rotate(which, strip, own, other, left, blocks):
    states = own.shape[2]
    rows = strip.shape[0] * strip.shape[3]
    vmem = pl.BlockSpec(memory_space=pltpu.VMEM)
    params = pltpu.CompilerParams(vmem_limit_bytes=40 * 1024 * 1024)
    near = pl.pallas_call(
        near_kernel,
        out_shape=jax.ShapeDtypeStruct((2, rows, states), F32),
        in_specs=[pl.BlockSpec(memory_space=pltpu.SMEM), vmem, vmem],
        out_specs=vmem,
        compiler_params=params,
        cost_estimate=pl.CostEstimate(flops=10**9, bytes_accessed=4 * 10**6, transcendentals=0),
    )(which, strip, own)
    return pl.pallas_call(
        rotate_kernel,
        out_shape=jax.ShapeDtypeStruct((blocks, 2, states // blocks, states), F32),
        in_specs=[pl.BlockSpec(memory_space=pltpu.SMEM), vmem, vmem, vmem, vmem],
        out_specs=vmem,
        compiler_params=params,
        cost_estimate=pl.CostEstimate(flops=3 * 10**9, bytes_accessed=6 * 10**6, transcendentals=0),
    )(which, strip, near, other, left)


def turn_kernel(value_ref, out_ref):
    rows = value_ref.shape[0]
    blocks = out_ref.shape[0]
    width = value_ref.shape[1] // (2 * blocks)
    turned = value_ref[...].T
    for index in range(2 * blocks):
        half = (index % 2) * rows
        out_ref[index // 2, 0:width, half : half + rows] = turned[index * width : (index + 1) * width]


def turn_columns(value, blocks):
    vmem = pl.BlockSpec(memory_space=pltpu.VMEM)
    return pl.pallas_call(
        turn_kernel,
        out_shape=jax.ShapeDtypeStruct((blocks, value.shape[1] // (2 * blocks), 2 * value.shape[0]), F32),
        in_specs=[vmem],
        out_specs=vmem,
    )(value)


def hermitize_kernel(place_ref, own_ref, *refs):
    pieces, out_ref, mirror_ref = refs[:-2], refs[-2], refs[-1]
    size = own_ref.shape[2]
    height = pieces[0].shape[2]
    for index, piece in enumerate(pieces):
        at = pl.multiple_of(place_ref[index] * height, height)
        mirror_ref[pl.ds(at, height), :] = piece[0, 0]
    step = 256
    diagonal = lax.broadcasted_iota(jnp.int32, (step, step), 0) == lax.broadcasted_iota(
        jnp.int32, (step, step), 1
    )
    identity = jnp.where(diagonal, 1.0, 0.0).astype(BF16)
    sign = jnp.where(pl.program_id(0) == 0, 1.0, -1.0).astype(F32)
    for down in range(0, size, step):
        for across in range(0, size, step):
            tile = mirror_ref[across : across + step, down : down + step]
            turned = contract(identity, tile, ((1,), (1,)))
            own = own_ref[0, down : down + step, across : across + step].astype(F32)
            out_ref[0, down : down + step, across : across + step] = (0.5 * (own + sign * turned)).astype(BF16)


def hermitize(place, sigma, pieces):
    _, _, width = sigma.shape
    factor, _, height, _ = pieces[0].shape
    tile = pl.BlockSpec((1, width, width), lambda part, half: (part, half, 0))
    piece = pl.BlockSpec((1, 1, height, width), lambda part, half: (half, part, 0, 0))
    return pl.pallas_call(
        hermitize_kernel,
        grid=(2, factor),
        out_shape=jax.ShapeDtypeStruct(sigma.shape, BF16),
        in_specs=[pl.BlockSpec(memory_space=pltpu.SMEM), tile] + [piece] * len(pieces),
        out_specs=tile,
        scratch_shapes=[pltpu.VMEM((width, width), BF16)],
        compiler_params=pltpu.CompilerParams(vmem_limit_bytes=32 * 1024 * 1024),
        cost_estimate=pl.CostEstimate(flops=10**9, bytes_accessed=6 * 10**6, transcendentals=0),
    )(place, sigma, *pieces)


def body(sigma, coeffs):
    row_count = lax.axis_size("row")
    col_count = lax.axis_size("col")
    states = coeffs.shape[2]
    factor = col_count // row_count
    depth = col_count // factor
    spread = row_count // 2
    _, tile_height, tile_width = sigma.shape
    strip_rows = tile_width // spread
    shard_rows = tile_width // row_count
    row = lax.axis_index("row")
    col = lax.axis_index("col")
    side = col % factor
    both = ("row", "col")

    def device(r, z, low):
        return r * col_count + factor * z + low

    everyone = [(r, z, low) for r in range(row_count) for z in range(depth) for low in range(factor)]
    plane = [
        [device(2 * m + core, z, low) for m in range(spread) for low in range(factor)]
        for core in range(2)
        for z in range(depth)
    ]
    along_z = [[factor * z + low for z in range(depth)] for low in range(factor)]
    swap = [(c, c ^ 1) for c in range(col_count)]

    turn = [
        (device(r, z, low), device(r - r % 2 + z % 2, z - z % 2 + r % 2, low)) for r, z, low in everyone
    ]
    left = lax.dynamic_slice_in_dim(coeffs, row * shard_rows, shard_rows, 1)
    left = lax.ppermute(left, both, turn)
    other = lax.ppermute(coeffs, "col", swap)

    moving = sigma.reshape(2, factor, spread, strip_rows, tile_width).transpose(2, 1, 0, 3, 4)
    moving = moving.reshape(spread * factor, 2, strip_rows, tile_width)
    moving, left = lax.optimization_barrier((moving, left))
    moving = lax.all_to_all(moving, both, 0, 0, tiled=True, axis_index_groups=plane)
    left = lax.all_gather(left, "col", axis=0, tiled=True, axis_index_groups=along_z)
    moving, left = lax.optimization_barrier((moving, left))
    left = left.reshape(depth, 2, shard_rows, states)
    strip = moving.reshape(spread, factor, 2, strip_rows, tile_width)

    first_strip = strip
    strip = lax.optimization_barrier(strip)
    chosen = []
    routes = []
    places = []
    for offset in ORDER:

        def target(r, z):
            return (r // 2 + STRIDE * z + offset) % spread

        route = [
            (device(r, z, low), device(z, 2 * target(r, z) + r % 2, low)) for r, z, low in everyone
        ]
        source = strip if chosen else first_strip
        chosen.append(lax.dynamic_index_in_dim(source, target(row, col // factor), 0, keepdims=False))
        routes.append(route)
        places.append((col // (2 * factor) - STRIDE * row - offset) % spread)

    term = rotate(side.astype(jnp.int32).reshape(1), strip, coeffs, other, left, row_count)
    term = lax.all_to_all(term, "row", 0, 0, tiled=True).sum(0)
    height, length = states // row_count, states // col_count
    term = turn_columns(term.reshape(2 * height, states), col_count)
    chosen[-1], term = lax.optimization_barrier((chosen[-1], term))
    pieces = [lax.ppermute(value, both, route) for value, route in zip(chosen, routes)]
    term = lax.all_to_all(term, "col", 0, 0, tiled=True)

    term = term.sum(0)
    term = jnp.concatenate([term[:, : 2 * height], term[:, 2 * height : 4 * height]], axis=0)
    rotated = term.T.reshape(2, height, length)

    hamiltonian = hermitize(jnp.stack(places).astype(jnp.int32), sigma, pieces)
    return (hamiltonian, rotated)


def solution(mesh):
    in_specs = (P(None, "row", "col"), P(None, "col", None))
    out_specs = (P(None, "row", "col"), P(None, "row", "col"))
    return jax.shard_map(body, mesh=mesh, in_specs=in_specs, out_specs=out_specs, check_vma=False)
```

time: 841 us -> 193 us (0.23)
  waiting for transfers between devices: 548 us -> 15.7 us
  blocking collectives: 205 us -> 42.4 us
  starting transfers between devices: 4.67 us -> 107 us
  local copies, waits for them, and re-layouts: 32.5 us -> 8.36 us
  between operations: 15.5 us -> 0.97 us
  matrix products: 13.4 us -> 0 us
  Pallas kernels: 0 us -> 12.4 us
  other arithmetic: 13.2 us -> 2.02 us
    psum x1 -> x0, waiting for transfers between devices: 293 us -> none  [spread(): return lax.psum(block, axis)]
    unnamed x3 -> x0, waiting for transfers between devices: 255 us -> none
    all_to_all x2 -> x0, blocking collectives: 149 us -> none  [the longest x1 115 us: move_columns(): lax.all_to_all(moving, 'col', split_axis=3, concat_axis=3, tiled=True)]
    ppermute x0 -> x10, starting transfers between devices: none -> 86.9 us  [the longest x8 82.9 us: body(): lax.ppermute(value, both, route)]
    unnamed x1 -> x0, blocking collectives: 55.8 us -> none
    all_gather x0 -> x1, blocking collectives: none -> 42.4 us  [body(): lax.all_gather(left, 'col', axis=0, tiled=True, axis_index_groups=along_z)]
    all_to_all x1 -> x3, starting transfers between devices: 4.59 us -> 20.4 us  [the longest x1 9.57 us: body(): lax.all_to_all(moving, both, 0, 0, tiled=True, axis_index_groups=plane)]
    ppermute x0 -> x10, waiting for transfers between devices: none -> 14.5 us  [the longest x8 14.4 us: body(): lax.ppermute(value, both, route)]
  transfers between devices with their start and end apart: 3 -> 13, of which waited for: 2 -> 3; matrix products, arithmetic and copies ran while one was open for 2% -> 4% of each run, Pallas kernels for 0% -> 3%
where the time goes in v2:
time: 193 us; the launch traced here: 189 us
  starting transfers between devices  107 us (55%)
  blocking collectives  42.4 us (22%)
  waiting for transfers between devices  15.7 us (8%)
  Pallas kernels  12.4 us (6%)
  local copies, waits for them, and re-layouts  8.36 us (4%)
  other arithmetic  2.02 us (1%)
    ppermute x8, starting transfers between devices, body(): lax.ppermute(value, both, route)  82.9 us
    all_gather x1, blocking collectives, body(): lax.all_gather(left, 'col', axis=0, tiled=True, axis_index_groups=along_z)  42.4 us
    ppermute x8, waiting for transfers between devices, body(): lax.ppermute(value, both, route)  14.4 us
    all_to_all x1, starting transfers between devices, body(): lax.all_to_all(moving, both, 0, 0, tiled=True, axis_index_groups=plane)  9.57 us
    all_to_all x1, starting transfers between devices, body(): term = lax.all_to_all(term, 'row', 0, 0, tiled=True).sum(0)  6.93 us
    pallas_call x1, Pallas kernels, rotate(): pl.pallas_call(rotate_kernel, out_shape=jax.ShapeDtypeStruct((blocks, 2,...  6 us
  transfers between devices with their start and end apart: 13, of which 3 were waited for; matrix products, arithmetic and copies ran while one was open for 4% of the time, Pallas kernels for 3%

profile of v2, /device:TPU:6, one launch (start us, length us, event | category | flops | bytes accessed | tf_op | source)
XLA Modules:
  0.0 189.1 jit_solution(3619165508175572223)
XLA Ops:
  0.6 0.8 constant_dynamic-slice_fusion
  1.4 0.7 collective-permute-start
  2.1 3.1 %copy.5 = bf16[8,2,2,64,512]{4,3,2,1,0:T(8,128)(2,1)} copy(bf16[8,2,2,64,512]{4,3,0,1,2:T(8,128)(2,1)} %bitcast.40) | data formatting | bytes 4194304 | tf_op jit(solution)/shard_map/transpose | solution.py:182
  5.2 0.0 collective-permute-done
  5.2 0.0 copy-start.1
  5.2 9.6 %all-to-all-start = ((bf16[16,2,64,512]{3,2,1,0:T(8,128)(2,1)}), bf16[16,2,64,512]{3,2,1,0:T(8,128)(2,1)S(1)}, u32[]{:S(2)}, u32[]{:S(2)}) async-start(bf16[16,2,64,512]{3,2,1,0:T(8,128)(2,1)} %bitcast.42), calls=%async_computation | async-start | bytes 4194304 | tf_op jit(solution)/shard_map/all_to_all | solution.py:185
  14.8 0.0 copy-done.1
  14.8 3.4 %collective-permute-start.8 = (bf16[2,512,384]{2,1,0:T(8,128)(2,1)S(1)}, bf16[2,512,384]{2,1,0:T(8,128)(2,1)}, u32[]{:S(2)}, u32[]{:S(2)}) collective-permute-start(bf16[2,512,384]{2,1,0:T(8,128)(2,1)S(1)} %copy-done.1), channel_id=1, source_target_pairs={{0,1},{1,0},{2,3},{3,2},{4,5},{5,4},{6,7},{7,6},{8,9},{9,8},{10,11... | collective-permute-start | bytes 2359304 | tf_op jit(solution)/shard_map/ppermute | solution.py:180
  18.2 42.4 %all_gather.3 = bf16[32,32,384]{2,1,0:T(8,128)(2,1)} all-gather(bf16[2,32,384]{2,1,0:T(8,128)(2,1)S(1)} %collective-permute-done), channel_id=1, replica_groups={{0,2,4,6,8,10,12,14,16,18,20,22,24,26,28,30},{1,3,5,7,9,11,13,15,17,19,..., dimensions={0}, use_global_device_ids=true | all-gather | bytes 835584 | tf_op jit(solution)/shard_map/all_gather | solution.py:186
  60.6 0.0 all-to-all-done
  60.6 0.0 copy-start.2
  60.6 1.3 shard_map.41.near_ref
  61.8 0.0 collective-permute-done.8.other_ref
  61.9 0.0 copy-done.2
  61.9 6.0 %shard_map.42 = f32[16,2,24,384]{3,2,1,0:T(8,128)} custom-call(s32[1]{0:T(128)} %bitcast.20.which_ref, bf16[8,2,2,64,512]{4,3,2,1,0:T(8,128)(2,1)S(1)} %bitcast.37, f32[2,512,384]{2,1,0:T(8,128)S(1)} %shard_map.41.near_ref, bf16[2,512,384]{2,1,0:T(8,128)(2,1)} %collective-permute-done.8.other_ref, bf16[16,2,32,384]{3,2,1,0:T(8,128)(2,1)S(1)} %bitcast.41), custom_call_target="tpu_custom_call" | custom-call | flops 3000000000 | bytes 6000000 | tf_op jit(solution)/shard_map/pallas_call | solution.py:80
  67.9 6.9 %all-to-all-start.1 = ((f32[16,2,24,384]{3,2,1,0:T(8,128)}), f32[16,2,24,384]{3,2,1,0:T(8,128)}, u32[]{:S(2)}, u32[]{:S(2)}) async-start(f32[16,2,24,384]{3,2,1,0:T(8,128)} %shard_map.42), calls=%async_computation.1 | async-start | bytes 2359296 | tf_op jit(solution)/shard_map/all_to_all | solution.py:210
  74.8 1.2 dynamic-slice_bitcast_fusion
  76.0 2.8 %collective-permute-start.2 = (bf16[2,2,64,512]{3,2,1,0:T(8,128)(2,1)}, bf16[2,2,64,512]{3,2,1,0:T(8,128)(2,1)S(1)}, u32[]{:S(2)}, u32[]{:S(2)}) collective-permute-start(bf16[2,2,64,512]{3,2,1,0:T(8,128)(2,1)} %get-tuple-element.20), channel_id=1, source_target_pairs={{0,16},{1,17},{2,36},{3,37},{4,88},{5,89},{6,108},{7,109},{8,128},... | collective-permute-start | bytes 786440 | tf_op jit(solution)/shard_map/ppermute | solution.py:214
  78.9 8.3 %collective-permute-start.3 = (bf16[2,2,64,512]{3,2,1,0:T(8,128)(2,1)}, bf16[2,2,64,512]{3,2,1,0:T(8,128)(2,1)S(1)}, u32[]{:S(2)}, u32[]{:S(2)}) collective-permute-start(bf16[2,2,64,512]{3,2,1,0:T(8,128)(2,1)} %get-tuple-element.19), channel_id=1, source_target_pairs={{0,8},{1,9},{2,60},{3,61},{4,80},{5,81},{6,100},{7,101},{8,152},{9... | collective-permute-start | bytes 786440 | tf_op jit(solution)/shard_map/ppermute | solution.py:214
  87.2 9.9 %collective-permute-start.4 = (bf16[2,2,64,512]{3,2,1,0:T(8,128)(2,1)}, bf16[2,2,64,512]{3,2,1,0:T(8,128)(2,1)S(1)}, u32[]{:S(2)}, u32[]{:S(2)}) collective-permute-start(bf16[2,2,64,512]{3,2,1,0:T(8,128)(2,1)} %get-tuple-element.18), channel_id=1, source_target_pairs={{0,24},{1,25},{2,44},{3,45},{4,64},{5,65},{6,116},{7,117},{8,136},... | collective-permute-start | bytes 786440 | tf_op jit(solution)/shard_map/ppermute | solution.py:214
  97.2 4.4 %collective-permute-start.5 = (bf16[2,2,64,512]{3,2,1,0:T(8,128)(2,1)}, bf16[2,2,64,512]{3,2,1,0:T(8,128)(2,1)S(1)}, u32[]{:S(2)}, u32[]{:S(2)}) collective-permute-start(bf16[2,2,64,512]{3,2,1,0:T(8,128)(2,1)} %get-tuple-element.17), channel_id=1, source_target_pairs={{0,4},{1,5},{2,56},{3,57},{4,76},{5,77},{6,96},{7,97},{8,148},{9,1... | collective-permute-start | bytes 786440 | tf_op jit(solution)/shard_map/ppermute | solution.py:214
  101.6 6.1 %collective-permute-start.6 = (bf16[2,2,64,512]{3,2,1,0:T(8,128)(2,1)}, bf16[2,2,64,512]{3,2,1,0:T(8,128)(2,1)S(1)}, u32[]{:S(2)}, u32[]{:S(2)}) collective-permute-start(bf16[2,2,64,512]{3,2,1,0:T(8,128)(2,1)} %get-tuple-element.16), channel_id=1, source_target_pairs={{0,20},{1,21},{2,40},{3,41},{4,92},{5,93},{6,112},{7,113},{8,132},... | collective-permute-start | bytes 786440 | tf_op jit(solution)/shard_map/ppermute | solution.py:214
  107.7 0.7 dynamic-slice_bitcast_fusion.7
  108.4 0.0 all-to-all-done.1
  108.4 2.0 %reduce_sum.18 = f32[2,24,384]{2,1,0:T(8,128)} reduce(f32[16,2,24,384]{3,2,1,0:T(8,128)} %all-to-all-done.1, f32[]{:T(128)} %constant.207.clone.1), dimensions={0}, to_apply=%region_0.1 | reduce | flops 276480 | bytes 1253380 | tf_op jit(solution)/shard_map/reduce_sum | solution.py:210
  110.4 1.7 shard_map.43
  112.2 0.0 collective-permute-done.2.refs_1_
  112.2 4.8 %collective-permute-start.7 = (bf16[2,2,64,512]{3,2,1,0:T(8,128)(2,1)}, bf16[2,2,64,512]{3,2,1,0:T(8,128)(2,1)S(1)}, u32[]{:S(2)}, u32[]{:S(2)}) collective-permute-start(bf16[2,2,64,512]{3,2,1,0:T(8,128)(2,1)} %get-tuple-element.15), channel_id=1, source_target_pairs={{0,12},{1,13},{2,32},{3,33},{4,84},{5,85},{6,104},{7,105},{8,156},... | collective-permute-start | bytes 786440 | tf_op jit(solution)/shard_map/ppermute | solution.py:214
  117.0 0.0 collective-permute-done.3.refs_2_
  117.0 22.9 %collective-permute-start.1 = (bf16[2,2,64,512]{3,2,1,0:T(8,128)(2,1)}, bf16[2,2,64,512]{3,2,1,0:T(8,128)(2,1)S(1)}, u32[]{:S(2)}, u32[]{:S(2)}) collective-permute-start(bf16[2,2,64,512]{3,2,1,0:T(8,128)(2,1)} %dynamic-slice_bitcast_fusion.7), channel_id=1, source_target_pairs={{0,0},{1,1},{2,52},{3,53},{4,72},{5,73},{6,124},{7,125},{8,144},{9... | collective-permute-start | bytes 786440 | tf_op jit(solution)/shard_map/ppermute | solution.py:214
  139.9 0.0 collective-permute-done.4.refs_3_
  139.9 23.6 %collective-permute-start.9 = (bf16[2,2,64,512]{3,2,1,0:T(8,128)(2,1)}, bf16[2,2,64,512]{3,2,1,0:T(8,128)(2,1)S(1)}, u32[]{:S(2)}, u32[]{:S(2)}) collective-permute-start(bf16[2,2,64,512]{3,2,1,0:T(8,128)(2,1)} %get-tuple-element.12), channel_id=1, source_target_pairs={{0,28},{1,29},{2,48},{3,49},{4,68},{5,69},{6,120},{7,121},{8,140},... | collective-permute-start | bytes 786440 | tf_op jit(solution)/shard_map/ppermute | solution.py:214
  163.5 3.9 %all-to-all-start.2 = ((f32[32,6,96]{2,1,0:T(8,128)}), f32[32,6,96]{2,1,0:T(8,128)S(1)}, u32[]{:S(2)}, u32[]{:S(2)}) async-start(f32[32,6,96]{2,1,0:T(8,128)} %shard_map.43), calls=%async_computation.2 | async-start | bytes 262144 | tf_op jit(solution)/shard_map/all_to_all | solution.py:215
  167.5 0.1 stack.35.place_ref
  167.6 0.0 collective-permute-done.5.refs_4_
  167.6 0.0 collective-permute-done.6.refs_5_
  167.6 0.0 collective-permute-done.7.refs_6_
  167.6 4.1 %collective-permute-done.1.refs_0_ = bf16[2,2,64,512]{3,2,1,0:T(8,128)(2,1)S(1)} collective-permute-done((bf16[2,2,64,512]{3,2,1,0:T(8,128)(2,1)}, bf16[2,2,64,512]{3,2,1,0:T(8,128)(2,1)S(1)}, u32[]{:S(2)}, u32[]{:S(2)}) %collective-permute-start.1) | collective-permute-done | bytes 262176 | tf_op jit(solution)/shard_map/ppermute | solution.py:214
  171.8 10.3 %collective-permute-done.9.refs_7_ = bf16[2,2,64,512]{3,2,1,0:T(8,128)(2,1)S(1)} collective-permute-done((bf16[2,2,64,512]{3,2,1,0:T(8,128)(2,1)}, bf16[2,2,64,512]{3,2,1,0:T(8,128)(2,1)S(1)}, u32[]{:S(2)}, u32[]{:S(2)}) %collective-permute-start.9) | collective-permute-done | bytes 262176 | tf_op jit(solution)/shard_map/ppermute | solution.py:214
  182.1 0.0 copy-start
  182.1 1.6 copy-done
  183.7 3.4 %shard_map.44 = bf16[2,1024,512]{2,1,0:T(8,128)(2,1)} custom-call(s32[8]{0:T(128)S(1)} %stack.35.place_ref, bf16[2,1024,512]{2,1,0:T(8,128)(2,1)S(1)} %copy-done, bf16[2,2,64,512]{3,2,1,0:T(8,128)(2,1)S(1)} %collective-permute-done.1.refs_0_, bf16[2,2,64,512]{3,2,1,0:T(8,128)(2,1)S(1)} %collective-permute-done.2.refs_1_, ...), custom_call_target="tpu_custom_call" | custom-call | flops 1000000000 | bytes 6000000 | tf_op jit(solution)/shard_map/pallas_call | solution.py:136
  187.0 1.2 all-to-all-done.2
  188.3 0.1 fusion
  188.4 0.7 reshape.31
  (2 shorter events, 0.0 us)
Async XLA Ops:
  1.4 3.8 %collective-permute-start = (bf16[2,32,384]{2,1,0:T(8,128)(2,1)S(1)}, bf16[2,32,384]{2,1,0:T(8,128)(2,1)S(1)}, u32[]{:S(2)}, u32[]{:S(2)}) collective-permute-start(bf16[2,32,384]{2,1,0:T(8,128)(2,1)S(1)} %constant_dynamic-slice_fusion), channel_id=1, source_target_pairs={{0,0},{1,1},{2,32},{3,33},{4,4},{5,5},{6,36},{7,37},{8,8},{9,9},{1... | collective-permute-start | bytes 147464 | tf_op jit(solution)/shard_map/ppermute | solution.py:179
  5.2 9.6 %copy-start.1 = (bf16[2,512,384]{2,1,0:T(8,128)(2,1)S(1)}, bf16[2,512,384]{2,1,0:T(8,128)(2,1)}, u32[]{:S(2)}) copy-start(bf16[2,512,384]{2,1,0:T(8,128)(2,1)} %own_ref.2) | copy-start | bytes 2359300
  5.2 55.3 %all-to-all-start = ((bf16[16,2,64,512]{3,2,1,0:T(8,128)(2,1)}), bf16[16,2,64,512]{3,2,1,0:T(8,128)(2,1)S(1)}, u32[]{:S(2)}, u32[]{:S(2)}) async-start(bf16[16,2,64,512]{3,2,1,0:T(8,128)(2,1)} %bitcast.42), calls=%async_computation | async-start | bytes 4194304 | tf_op jit(solution)/shard_map/all_to_all | solution.py:185
  14.8 47.0 %collective-permute-start.8 = (bf16[2,512,384]{2,1,0:T(8,128)(2,1)S(1)}, bf16[2,512,384]{2,1,0:T(8,128)(2,1)}, u32[]{:S(2)}, u32[]{:S(2)}) collective-permute-start(bf16[2,512,384]{2,1,0:T(8,128)(2,1)S(1)} %copy-done.1), channel_id=1, source_target_pairs={{0,1},{1,0},{2,3},{3,2},{4,5},{5,4},{6,7},{7,6},{8,9},{9,8},{10,11... | collective-permute-start | bytes 2359304 | tf_op jit(solution)/shard_map/ppermute | solution.py:180
  60.6 1.3 copy-start.2
  67.9 40.6 %all-to-all-start.1 = ((f32[16,2,24,384]{3,2,1,0:T(8,128)}), f32[16,2,24,384]{3,2,1,0:T(8,128)}, u32[]{:S(2)}, u32[]{:S(2)}) async-start(f32[16,2,24,384]{3,2,1,0:T(8,128)} %shard_map.42), calls=%async_computation.1 | async-start | bytes 2359296 | tf_op jit(solution)/shard_map/all_to_all | solution.py:210
  76.0 36.1 %collective-permute-start.2 = (bf16[2,2,64,512]{3,2,1,0:T(8,128)(2,1)}, bf16[2,2,64,512]{3,2,1,0:T(8,128)(2,1)S(1)}, u32[]{:S(2)}, u32[]{:S(2)}) collective-permute-start(bf16[2,2,64,512]{3,2,1,0:T(8,128)(2,1)} %get-tuple-element.20), channel_id=1, source_target_pairs={{0,16},{1,17},{2,36},{3,37},{4,88},{5,89},{6,108},{7,109},{8,128},... | collective-permute-start | bytes 786440 | tf_op jit(solution)/shard_map/ppermute | solution.py:214
  78.9 38.1 %collective-permute-start.3 = (bf16[2,2,64,512]{3,2,1,0:T(8,128)(2,1)}, bf16[2,2,64,512]{3,2,1,0:T(8,128)(2,1)S(1)}, u32[]{:S(2)}, u32[]{:S(2)}) collective-permute-start(bf16[2,2,64,512]{3,2,1,0:T(8,128)(2,1)} %get-tuple-element.19), channel_id=1, source_target_pairs={{0,8},{1,9},{2,60},{3,61},{4,80},{5,81},{6,100},{7,101},{8,152},{9... | collective-permute-start | bytes 786440 | tf_op jit(solution)/shard_map/ppermute | solution.py:214
  87.2 52.7 %collective-permute-start.4 = (bf16[2,2,64,512]{3,2,1,0:T(8,128)(2,1)}, bf16[2,2,64,512]{3,2,1,0:T(8,128)(2,1)S(1)}, u32[]{:S(2)}, u32[]{:S(2)}) collective-permute-start(bf16[2,2,64,512]{3,2,1,0:T(8,128)(2,1)} %get-tuple-element.18), channel_id=1, source_target_pairs={{0,24},{1,25},{2,44},{3,45},{4,64},{5,65},{6,116},{7,117},{8,136},... | collective-permute-start | bytes 786440 | tf_op jit(solution)/shard_map/ppermute | solution.py:214
  97.2 70.4 %collective-permute-start.5 = (bf16[2,2,64,512]{3,2,1,0:T(8,128)(2,1)}, bf16[2,2,64,512]{3,2,1,0:T(8,128)(2,1)S(1)}, u32[]{:S(2)}, u32[]{:S(2)}) collective-permute-start(bf16[2,2,64,512]{3,2,1,0:T(8,128)(2,1)} %get-tuple-element.17), channel_id=1, source_target_pairs={{0,4},{1,5},{2,56},{3,57},{4,76},{5,77},{6,96},{7,97},{8,148},{9,1... | collective-permute-start | bytes 786440 | tf_op jit(solution)/shard_map/ppermute | solution.py:214
  101.6 66.0 %collective-permute-start.6 = (bf16[2,2,64,512]{3,2,1,0:T(8,128)(2,1)}, bf16[2,2,64,512]{3,2,1,0:T(8,128)(2,1)S(1)}, u32[]{:S(2)}, u32[]{:S(2)}) collective-permute-start(bf16[2,2,64,512]{3,2,1,0:T(8,128)(2,1)} %get-tuple-element.16), channel_id=1, source_target_pairs={{0,20},{1,21},{2,40},{3,41},{4,92},{5,93},{6,112},{7,113},{8,132},... | collective-permute-start | bytes 786440 | tf_op jit(solution)/shard_map/ppermute | solution.py:214
  112.2 55.5 %collective-permute-start.7 = (bf16[2,2,64,512]{3,2,1,0:T(8,128)(2,1)}, bf16[2,2,64,512]{3,2,1,0:T(8,128)(2,1)S(1)}, u32[]{:S(2)}, u32[]{:S(2)}) collective-permute-start(bf16[2,2,64,512]{3,2,1,0:T(8,128)(2,1)} %get-tuple-element.15), channel_id=1, source_target_pairs={{0,12},{1,13},{2,32},{3,33},{4,84},{5,85},{6,104},{7,105},{8,156},... | collective-permute-start | bytes 786440 | tf_op jit(solution)/shard_map/ppermute | solution.py:214
  117.0 54.7 %collective-permute-start.1 = (bf16[2,2,64,512]{3,2,1,0:T(8,128)(2,1)}, bf16[2,2,64,512]{3,2,1,0:T(8,128)(2,1)S(1)}, u32[]{:S(2)}, u32[]{:S(2)}) collective-permute-start(bf16[2,2,64,512]{3,2,1,0:T(8,128)(2,1)} %dynamic-slice_bitcast_fusion.7), channel_id=1, source_target_pairs={{0,0},{1,1},{2,52},{3,53},{4,72},{5,73},{6,124},{7,125},{8,144},{9... | collective-permute-start | bytes 786440 | tf_op jit(solution)/shard_map/ppermute | solution.py:214
  139.9 42.2 %collective-permute-start.9 = (bf16[2,2,64,512]{3,2,1,0:T(8,128)(2,1)}, bf16[2,2,64,512]{3,2,1,0:T(8,128)(2,1)S(1)}, u32[]{:S(2)}, u32[]{:S(2)}) collective-permute-start(bf16[2,2,64,512]{3,2,1,0:T(8,128)(2,1)} %get-tuple-element.12), channel_id=1, source_target_pairs={{0,28},{1,29},{2,48},{3,49},{4,68},{5,69},{6,120},{7,121},{8,140},... | collective-permute-start | bytes 786440 | tf_op jit(solution)/shard_map/ppermute | solution.py:214
  163.5 24.7 %all-to-all-start.2 = ((f32[32,6,96]{2,1,0:T(8,128)}), f32[32,6,96]{2,1,0:T(8,128)S(1)}, u32[]{:S(2)}, u32[]{:S(2)}) async-start(f32[32,6,96]{2,1,0:T(8,128)} %shard_map.43), calls=%async_computation.2 | async-start | bytes 262144 | tf_op jit(solution)/shard_map/all_to_all | solution.py:215
  182.1 1.6 copy-start

commit v3 on v2

--- a/solution.py
+++ b/solution.py
@@ -170,14 +170,14 @@
         for z in range(depth)
     ]
     along_z = [[factor * z + low for z in range(depth)] for low in range(factor)]
-    swap = [(c, c ^ 1) for c in range(col_count)]
+    swap = [(device(r, z, low), device(r ^ (2 * (r % 2)), z, low ^ 1)) for r, z, low in everyone]
 
     turn = [
         (device(r, z, low), device(r - r % 2 + z % 2, z - z % 2 + r % 2, low)) for r, z, low in everyone
     ]
     left = lax.dynamic_slice_in_dim(coeffs, row * shard_rows, shard_rows, 1)
     left = lax.ppermute(left, both, turn)
-    other = lax.ppermute(coeffs, "col", swap)
+    other = lax.ppermute(coeffs, both, swap)
 
     moving = sigma.reshape(2, factor, spread, strip_rows, tile_width).transpose(2, 1, 0, 3, 4)
     moving = moving.reshape(spread * factor, 2, strip_rows, tile_width)

time: 193 us -> 190 us (0.984); the launches traced: 189 us -> 189 us
  waiting for transfers between devices: 15.7 us -> 35.1 us
  starting transfers between devices: 107 us -> 88.6 us
    ppermute x8, waiting for transfers between devices: 14.4 us -> 35.1 us  [body(): lax.ppermute(value, both, route)]
    ppermute x8, starting transfers between devices: 82.9 us -> 63.9 us  [body(): lax.ppermute(value, both, route)]
where the time goes in v3:
time: 190 us; the launch traced here: 189 us
  starting transfers between devices  88.6 us (47%)
  blocking collectives  41.8 us (22%)
  waiting for transfers between devices  35.1 us (18%)
  Pallas kernels  12.4 us (7%)
  local copies, waits for them, and re-layouts  8.36 us (4%)
  other arithmetic  2.02 us (1%)
    ppermute x8, starting transfers between devices, body(): lax.ppermute(value, both, route)  63.9 us
    all_gather x1, blocking collectives, body(): lax.all_gather(left, 'col', axis=0, tiled=True, axis_index_groups=along_z)  41.8 us
    ppermute x8, waiting for transfers between devices, body(): lax.ppermute(value, both, route)  35.1 us
    all_to_all x1, starting transfers between devices, body(): lax.all_to_all(moving, both, 0, 0, tiled=True, axis_index_groups=plane)  9.57 us
    all_to_all x1, starting transfers between devices, body(): term = lax.all_to_all(term, 'row', 0, 0, tiled=True).sum(0)  7.25 us
    pallas_call x1, Pallas kernels, rotate(): pl.pallas_call(rotate_kernel, out_shape=jax.ShapeDtypeStruct((blocks, 2,...  6 us
    all_to_all x1, starting transfers between devices, body(): term = lax.all_to_all(term, 'col', 0, 0, tiled=True)  3.86 us
  transfers between devices with their start and end apart: 13, of which 3 were waited for; matrix products, arithmetic and copies ran while one was open for 4% of the time, Pallas kernels for 3%

profile of v3, /device:TPU:6, one launch (start us, length us, event | category | flops | bytes accessed | tf_op | source)
XLA Modules:
  0.0 189.2 jit_solution(11813150138461418425)
XLA Ops:
  0.6 0.8 constant_dynamic-slice_fusion
  1.4 0.7 collective-permute-start
  2.1 3.1 %copy.5 = bf16[8,2,2,64,512]{4,3,2,1,0:T(8,128)(2,1)} copy(bf16[8,2,2,64,512]{4,3,0,1,2:T(8,128)(2,1)} %bitcast.40) | data formatting | bytes 4194304 | tf_op jit(solution)/shard_map/transpose | solution.py:182
  5.2 0.0 collective-permute-done
  5.2 0.0 copy-start.1
  5.2 9.6 %all-to-all-start = ((bf16[16,2,64,512]{3,2,1,0:T(8,128)(2,1)}), bf16[16,2,64,512]{3,2,1,0:T(8,128)(2,1)S(1)}, u32[]{:S(2)}, u32[]{:S(2)}) async-start(bf16[16,2,64,512]{3,2,1,0:T(8,128)(2,1)} %bitcast.42), calls=%async_computation | async-start | bytes 4194304 | tf_op jit(solution)/shard_map/all_to_all | solution.py:185
  14.8 0.0 copy-done.1
  14.8 3.4 %collective-permute-start.8 = (bf16[2,512,384]{2,1,0:T(8,128)(2,1)S(1)}, bf16[2,512,384]{2,1,0:T(8,128)(2,1)}, u32[]{:S(2)}, u32[]{:S(2)}) collective-permute-start(bf16[2,512,384]{2,1,0:T(8,128)(2,1)S(1)} %copy-done.1), channel_id=1, source_target_pairs={{0,1},{1,0},{2,3},{3,2},{4,5},{5,4},{6,7},{7,6},{8,9},{9,8},{10,11... | collective-permute-start | bytes 2359304 | tf_op jit(solution)/shard_map/ppermute | solution.py:180
  18.2 41.8 %all_gather.3 = bf16[32,32,384]{2,1,0:T(8,128)(2,1)} all-gather(bf16[2,32,384]{2,1,0:T(8,128)(2,1)S(1)} %collective-permute-done), channel_id=1, replica_groups={{0,2,4,6,8,10,12,14,16,18,20,22,24,26,28,30},{1,3,5,7,9,11,13,15,17,19,..., dimensions={0}, use_global_device_ids=true | all-gather | bytes 835584 | tf_op jit(solution)/shard_map/all_gather | solution.py:186
  60.0 0.0 all-to-all-done
  60.0 0.0 copy-start.2
  60.0 1.3 shard_map.41.near_ref
  61.3 0.0 collective-permute-done.8.other_ref
  61.3 0.0 copy-done.2
  61.3 6.0 %shard_map.42 = f32[16,2,24,384]{3,2,1,0:T(8,128)} custom-call(s32[1]{0:T(128)} %bitcast.20.which_ref, bf16[8,2,2,64,512]{4,3,2,1,0:T(8,128)(2,1)S(1)} %bitcast.37, f32[2,512,384]{2,1,0:T(8,128)S(1)} %shard_map.41.near_ref, bf16[2,512,384]{2,1,0:T(8,128)(2,1)} %collective-permute-done.8.other_ref, bf16[16,2,32,384]{3,2,1,0:T(8,128)(2,1)S(1)} %bitcast.41), custom_call_target="tpu_custom_call" | custom-call | flops 3000000000 | bytes 6000000 | tf_op jit(solution)/shard_map/pallas_call | solution.py:80
  67.3 7.2 %all-to-all-start.1 = ((f32[16,2,24,384]{3,2,1,0:T(8,128)}), f32[16,2,24,384]{3,2,1,0:T(8,128)}, u32[]{:S(2)}, u32[]{:S(2)}) async-start(f32[16,2,24,384]{3,2,1,0:T(8,128)} %shard_map.42), calls=%async_computation.1 | async-start | bytes 2359296 | tf_op jit(solution)/shard_map/all_to_all | solution.py:210
  74.6 1.2 dynamic-slice_bitcast_fusion
  75.8 3.4 %collective-permute-start.2 = (bf16[2,2,64,512]{3,2,1,0:T(8,128)(2,1)}, bf16[2,2,64,512]{3,2,1,0:T(8,128)(2,1)S(1)}, u32[]{:S(2)}, u32[]{:S(2)}) collective-permute-start(bf16[2,2,64,512]{3,2,1,0:T(8,128)(2,1)} %get-tuple-element.20), channel_id=1, source_target_pairs={{0,16},{1,17},{2,36},{3,37},{4,88},{5,89},{6,108},{7,109},{8,128},... | collective-permute-start | bytes 786440 | tf_op jit(solution)/shard_map/ppermute | solution.py:214
  79.2 6.0 %collective-permute-start.3 = (bf16[2,2,64,512]{3,2,1,0:T(8,128)(2,1)}, bf16[2,2,64,512]{3,2,1,0:T(8,128)(2,1)S(1)}, u32[]{:S(2)}, u32[]{:S(2)}) collective-permute-start(bf16[2,2,64,512]{3,2,1,0:T(8,128)(2,1)} %get-tuple-element.19), channel_id=1, source_target_pairs={{0,8},{1,9},{2,60},{3,61},{4,80},{5,81},{6,100},{7,101},{8,152},{9... | collective-permute-start | bytes 786440 | tf_op jit(solution)/shard_map/ppermute | solution.py:214
  85.2 9.9 %collective-permute-start.4 = (bf16[2,2,64,512]{3,2,1,0:T(8,128)(2,1)}, bf16[2,2,64,512]{3,2,1,0:T(8,128)(2,1)S(1)}, u32[]{:S(2)}, u32[]{:S(2)}) collective-permute-start(bf16[2,2,64,512]{3,2,1,0:T(8,128)(2,1)} %get-tuple-element.18), channel_id=1, source_target_pairs={{0,24},{1,25},{2,44},{3,45},{4,64},{5,65},{6,116},{7,117},{8,136},... | collective-permute-start | bytes 786440 | tf_op jit(solution)/shard_map/ppermute | solution.py:214
  95.1 6.8 %collective-permute-start.5 = (bf16[2,2,64,512]{3,2,1,0:T(8,128)(2,1)}, bf16[2,2,64,512]{3,2,1,0:T(8,128)(2,1)S(1)}, u32[]{:S(2)}, u32[]{:S(2)}) collective-permute-start(bf16[2,2,64,512]{3,2,1,0:T(8,128)(2,1)} %get-tuple-element.17), channel_id=1, source_target_pairs={{0,4},{1,5},{2,56},{3,57},{4,76},{5,77},{6,96},{7,97},{8,148},{9,1... | collective-permute-start | bytes 786440 | tf_op jit(solution)/shard_map/ppermute | solution.py:214
  101.9 5.6 %collective-permute-start.6 = (bf16[2,2,64,512]{3,2,1,0:T(8,128)(2,1)}, bf16[2,2,64,512]{3,2,1,0:T(8,128)(2,1)S(1)}, u32[]{:S(2)}, u32[]{:S(2)}) collective-permute-start(bf16[2,2,64,512]{3,2,1,0:T(8,128)(2,1)} %get-tuple-element.16), channel_id=1, source_target_pairs={{0,20},{1,21},{2,40},{3,41},{4,92},{5,93},{6,112},{7,113},{8,132},... | collective-permute-start | bytes 786440 | tf_op jit(solution)/shard_map/ppermute | solution.py:214
  107.5 0.7 dynamic-slice_bitcast_fusion.7
  108.2 0.0 all-to-all-done.1
  108.2 2.0 %reduce_sum.18 = f32[2,24,384]{2,1,0:T(8,128)} reduce(f32[16,2,24,384]{3,2,1,0:T(8,128)} %all-to-all-done.1, f32[]{:T(128)} %constant.207.clone.1), dimensions={0}, to_apply=%region_0.1 | reduce | flops 276480 | bytes 1253380 | tf_op jit(solution)/shard_map/reduce_sum | solution.py:210
  110.2 1.7 shard_map.43
  111.9 0.0 collective-permute-done.2.refs_1_
  111.9 4.8 %collective-permute-start.7 = (bf16[2,2,64,512]{3,2,1,0:T(8,128)(2,1)}, bf16[2,2,64,512]{3,2,1,0:T(8,128)(2,1)S(1)}, u32[]{:S(2)}, u32[]{:S(2)}) collective-permute-start(bf16[2,2,64,512]{3,2,1,0:T(8,128)(2,1)} %get-tuple-element.15), channel_id=1, source_target_pairs={{0,12},{1,13},{2,32},{3,33},{4,84},{5,85},{6,104},{7,105},{8,156},... | collective-permute-start | bytes 786440 | tf_op jit(solution)/shard_map/ppermute | solution.py:214
  116.8 13.6 %collective-permute-done.3.refs_2_ = bf16[2,2,64,512]{3,2,1,0:T(8,128)(2,1)S(1)} collective-permute-done((bf16[2,2,64,512]{3,2,1,0:T(8,128)(2,1)}, bf16[2,2,64,512]{3,2,1,0:T(8,128)(2,1)S(1)}, u32[]{:S(2)}, u32[]{:S(2)}) %collective-permute-start.3) | collective-permute-done | bytes 262176 | tf_op jit(solution)/shard_map/ppermute | solution.py:214
  130.4 1.9 %collective-permute-start.1 = (bf16[2,2,64,512]{3,2,1,0:T(8,128)(2,1)}, bf16[2,2,64,512]{3,2,1,0:T(8,128)(2,1)S(1)}, u32[]{:S(2)}, u32[]{:S(2)}) collective-permute-start(bf16[2,2,64,512]{3,2,1,0:T(8,128)(2,1)} %dynamic-slice_bitcast_fusion.7), channel_id=1, source_target_pairs={{0,0},{1,1},{2,52},{3,53},{4,72},{5,73},{6,124},{7,125},{8,144},{9... | collective-permute-start | bytes 786440 | tf_op jit(solution)/shard_map/ppermute | solution.py:214
  132.3 0.0 collective-permute-done.4.refs_3_
  132.3 25.6 %collective-permute-start.9 = (bf16[2,2,64,512]{3,2,1,0:T(8,128)(2,1)}, bf16[2,2,64,512]{3,2,1,0:T(8,128)(2,1)S(1)}, u32[]{:S(2)}, u32[]{:S(2)}) collective-permute-start(bf16[2,2,64,512]{3,2,1,0:T(8,128)(2,1)} %get-tuple-element.12), channel_id=1, source_target_pairs={{0,28},{1,29},{2,48},{3,49},{4,68},{5,69},{6,120},{7,121},{8,140},... | collective-permute-start | bytes 786440 | tf_op jit(solution)/shard_map/ppermute | solution.py:214
  157.9 3.9 %all-to-all-start.2 = ((f32[32,6,96]{2,1,0:T(8,128)}), f32[32,6,96]{2,1,0:T(8,128)S(1)}, u32[]{:S(2)}, u32[]{:S(2)}) async-start(f32[32,6,96]{2,1,0:T(8,128)} %shard_map.43), calls=%async_computation.2 | async-start | bytes 262144 | tf_op jit(solution)/shard_map/all_to_all | solution.py:215
  161.9 0.1 stack.35.place_ref
  162.0 0.0 collective-permute-done.5.refs_4_
  162.0 0.0 collective-permute-done.6.refs_5_
  162.0 8.8 %collective-permute-done.7.refs_6_ = bf16[2,2,64,512]{3,2,1,0:T(8,128)(2,1)S(1)} collective-permute-done((bf16[2,2,64,512]{3,2,1,0:T(8,128)(2,1)}, bf16[2,2,64,512]{3,2,1,0:T(8,128)(2,1)S(1)}, u32[]{:S(2)}, u32[]{:S(2)}) %collective-permute-start.7) | collective-permute-done | bytes 262176 | tf_op jit(solution)/shard_map/ppermute | solution.py:214
  170.8 0.0 collective-permute-done.1.refs_0_
  170.8 12.7 %collective-permute-done.9.refs_7_ = bf16[2,2,64,512]{3,2,1,0:T(8,128)(2,1)S(1)} collective-permute-done((bf16[2,2,64,512]{3,2,1,0:T(8,128)(2,1)}, bf16[2,2,64,512]{3,2,1,0:T(8,128)(2,1)S(1)}, u32[]{:S(2)}, u32[]{:S(2)}) %collective-permute-start.9) | collective-permute-done | bytes 262176 | tf_op jit(solution)/shard_map/ppermute | solution.py:214
  183.5 0.0 copy-start
  183.5 1.6 copy-done
  185.1 3.4 %shard_map.44 = bf16[2,1024,512]{2,1,0:T(8,128)(2,1)} custom-call(s32[8]{0:T(128)S(1)} %stack.35.place_ref, bf16[2,1024,512]{2,1,0:T(8,128)(2,1)S(1)} %copy-done, bf16[2,2,64,512]{3,2,1,0:T(8,128)(2,1)S(1)} %collective-permute-done.1.refs_0_, bf16[2,2,64,512]{3,2,1,0:T(8,128)(2,1)S(1)} %collective-permute-done.2.refs_1_, ...), custom_call_target="tpu_custom_call" | custom-call | flops 1000000000 | bytes 6000000 | tf_op jit(solution)/shard_map/pallas_call | solution.py:136
  188.4 0.0 all-to-all-done.2
  188.5 0.1 fusion
  188.6 0.7 reshape.31
  (2 shorter events, 0.0 us)
Async XLA Ops:
  1.4 3.8 %collective-permute-start = (bf16[2,32,384]{2,1,0:T(8,128)(2,1)S(1)}, bf16[2,32,384]{2,1,0:T(8,128)(2,1)S(1)}, u32[]{:S(2)}, u32[]{:S(2)}) collective-permute-start(bf16[2,32,384]{2,1,0:T(8,128)(2,1)S(1)} %constant_dynamic-slice_fusion), channel_id=1, source_target_pairs={{0,0},{1,1},{2,32},{3,33},{4,4},{5,5},{6,36},{7,37},{8,8},{9,9},{1... | collective-permute-start | bytes 147464 | tf_op jit(solution)/shard_map/ppermute | solution.py:179
  5.2 9.6 %copy-start.1 = (bf16[2,512,384]{2,1,0:T(8,128)(2,1)S(1)}, bf16[2,512,384]{2,1,0:T(8,128)(2,1)}, u32[]{:S(2)}) copy-start(bf16[2,512,384]{2,1,0:T(8,128)(2,1)} %own_ref.2) | copy-start | bytes 2359300
  5.2 54.8 %all-to-all-start = ((bf16[16,2,64,512]{3,2,1,0:T(8,128)(2,1)}), bf16[16,2,64,512]{3,2,1,0:T(8,128)(2,1)S(1)}, u32[]{:S(2)}, u32[]{:S(2)}) async-start(bf16[16,2,64,512]{3,2,1,0:T(8,128)(2,1)} %bitcast.42), calls=%async_computation | async-start | bytes 4194304 | tf_op jit(solution)/shard_map/all_to_all | solution.py:185
  14.8 46.5 %collective-permute-start.8 = (bf16[2,512,384]{2,1,0:T(8,128)(2,1)S(1)}, bf16[2,512,384]{2,1,0:T(8,128)(2,1)}, u32[]{:S(2)}, u32[]{:S(2)}) collective-permute-start(bf16[2,512,384]{2,1,0:T(8,128)(2,1)S(1)} %copy-done.1), channel_id=1, source_target_pairs={{0,1},{1,0},{2,3},{3,2},{4,5},{5,4},{6,7},{7,6},{8,9},{9,8},{10,11... | collective-permute-start | bytes 2359304 | tf_op jit(solution)/shard_map/ppermute | solution.py:180
  60.0 1.3 copy-start.2
  67.3 40.9 %all-to-all-start.1 = ((f32[16,2,24,384]{3,2,1,0:T(8,128)}), f32[16,2,24,384]{3,2,1,0:T(8,128)}, u32[]{:S(2)}, u32[]{:S(2)}) async-start(f32[16,2,24,384]{3,2,1,0:T(8,128)} %shard_map.42), calls=%async_computation.1 | async-start | bytes 2359296 | tf_op jit(solution)/shard_map/all_to_all | solution.py:210
  75.8 36.1 %collective-permute-start.2 = (bf16[2,2,64,512]{3,2,1,0:T(8,128)(2,1)}, bf16[2,2,64,512]{3,2,1,0:T(8,128)(2,1)S(1)}, u32[]{:S(2)}, u32[]{:S(2)}) collective-permute-start(bf16[2,2,64,512]{3,2,1,0:T(8,128)(2,1)} %get-tuple-element.20), channel_id=1, source_target_pairs={{0,16},{1,17},{2,36},{3,37},{4,88},{5,89},{6,108},{7,109},{8,128},... | collective-permute-start | bytes 786440 | tf_op jit(solution)/shard_map/ppermute | solution.py:214
  79.2 51.2 %collective-permute-start.3 = (bf16[2,2,64,512]{3,2,1,0:T(8,128)(2,1)}, bf16[2,2,64,512]{3,2,1,0:T(8,128)(2,1)S(1)}, u32[]{:S(2)}, u32[]{:S(2)}) collective-permute-start(bf16[2,2,64,512]{3,2,1,0:T(8,128)(2,1)} %get-tuple-element.19), channel_id=1, source_target_pairs={{0,8},{1,9},{2,60},{3,61},{4,80},{5,81},{6,100},{7,101},{8,152},{9... | collective-permute-start | bytes 786440 | tf_op jit(solution)/shard_map/ppermute | solution.py:214
  85.2 47.1 %collective-permute-start.4 = (bf16[2,2,64,512]{3,2,1,0:T(8,128)(2,1)}, bf16[2,2,64,512]{3,2,1,0:T(8,128)(2,1)S(1)}, u32[]{:S(2)}, u32[]{:S(2)}) collective-permute-start(bf16[2,2,64,512]{3,2,1,0:T(8,128)(2,1)} %get-tuple-element.18), channel_id=1, source_target_pairs={{0,24},{1,25},{2,44},{3,45},{4,64},{5,65},{6,116},{7,117},{8,136},... | collective-permute-start | bytes 786440 | tf_op jit(solution)/shard_map/ppermute | solution.py:214
  95.1 66.8 %collective-permute-start.5 = (bf16[2,2,64,512]{3,2,1,0:T(8,128)(2,1)}, bf16[2,2,64,512]{3,2,1,0:T(8,128)(2,1)S(1)}, u32[]{:S(2)}, u32[]{:S(2)}) collective-permute-start(bf16[2,2,64,512]{3,2,1,0:T(8,128)(2,1)} %get-tuple-element.17), channel_id=1, source_target_pairs={{0,4},{1,5},{2,56},{3,57},{4,76},{5,77},{6,96},{7,97},{8,148},{9,1... | collective-permute-start | bytes 786440 | tf_op jit(solution)/shard_map/ppermute | solution.py:214
  101.9 60.1 %collective-permute-start.6 = (bf16[2,2,64,512]{3,2,1,0:T(8,128)(2,1)}, bf16[2,2,64,512]{3,2,1,0:T(8,128)(2,1)S(1)}, u32[]{:S(2)}, u32[]{:S(2)}) collective-permute-start(bf16[2,2,64,512]{3,2,1,0:T(8,128)(2,1)} %get-tuple-element.16), channel_id=1, source_target_pairs={{0,20},{1,21},{2,40},{3,41},{4,92},{5,93},{6,112},{7,113},{8,132},... | collective-permute-start | bytes 786440 | tf_op jit(solution)/shard_map/ppermute | solution.py:214
  111.9 58.9 %collective-permute-start.7 = (bf16[2,2,64,512]{3,2,1,0:T(8,128)(2,1)}, bf16[2,2,64,512]{3,2,1,0:T(8,128)(2,1)S(1)}, u32[]{:S(2)}, u32[]{:S(2)}) collective-permute-start(bf16[2,2,64,512]{3,2,1,0:T(8,128)(2,1)} %get-tuple-element.15), channel_id=1, source_target_pairs={{0,12},{1,13},{2,32},{3,33},{4,84},{5,85},{6,104},{7,105},{8,156},... | collective-permute-start | bytes 786440 | tf_op jit(solution)/shard_map/ppermute | solution.py:214
  130.4 40.5 %collective-permute-start.1 = (bf16[2,2,64,512]{3,2,1,0:T(8,128)(2,1)}, bf16[2,2,64,512]{3,2,1,0:T(8,128)(2,1)S(1)}, u32[]{:S(2)}, u32[]{:S(2)}) collective-permute-start(bf16[2,2,64,512]{3,2,1,0:T(8,128)(2,1)} %dynamic-slice_bitcast_fusion.7), channel_id=1, source_target_pairs={{0,0},{1,1},{2,52},{3,53},{4,72},{5,73},{6,124},{7,125},{8,144},{9... | collective-permute-start | bytes 786440 | tf_op jit(solution)/shard_map/ppermute | solution.py:214
  132.3 51.2 %collective-permute-start.9 = (bf16[2,2,64,512]{3,2,1,0:T(8,128)(2,1)}, bf16[2,2,64,512]{3,2,1,0:T(8,128)(2,1)S(1)}, u32[]{:S(2)}, u32[]{:S(2)}) collective-permute-start(bf16[2,2,64,512]{3,2,1,0:T(8,128)(2,1)} %get-tuple-element.12), channel_id=1, source_target_pairs={{0,28},{1,29},{2,48},{3,49},{4,68},{5,69},{6,120},{7,121},{8,140},... | collective-permute-start | bytes 786440 | tf_op jit(solution)/shard_map/ppermute | solution.py:214
  157.9 30.6 %all-to-all-start.2 = ((f32[32,6,96]{2,1,0:T(8,128)}), f32[32,6,96]{2,1,0:T(8,128)S(1)}, u32[]{:S(2)}, u32[]{:S(2)}) async-start(f32[32,6,96]{2,1,0:T(8,128)} %shard_map.43), calls=%async_computation.2 | async-start | bytes 262144 | tf_op jit(solution)/shard_map/all_to_all | solution.py:215
  183.5 1.6 copy-start

commit v4 on v3

--- a/solution.py
+++ b/solution.py
@@ -145,6 +145,31 @@
     )(place, sigma, *pieces)
 
 
+def strips_kernel(tile_ref, out_ref, done):
+    parts, factor = tile_ref.shape[:2]
+    copies = [
+        pltpu.make_async_copy(tile_ref.at[part, half], out_ref.at[:, half, part], done.at[part, half])
+        for part in range(parts)
+        for half in range(factor)
+    ]
+    for copy in copies:
+        copy.start()
+    for copy in copies:
+        copy.wait()
+
+
+def strips(tile):
+    parts, factor, count, rows, columns = tile.shape
+    return pl.pallas_call(
+        strips_kernel,
+        out_shape=jax.ShapeDtypeStruct((count, factor, parts, rows, columns), BF16),
+        in_specs=[pl.BlockSpec(memory_space=pl.ANY)],
+        out_specs=pl.BlockSpec(memory_space=pl.ANY),
+        scratch_shapes=[pltpu.SemaphoreType.DMA((parts, factor))],
+        cost_estimate=pl.CostEstimate(flops=0, bytes_accessed=4 * 10**6, transcendentals=0),
+    )(tile)
+
+
 def body(sigma, coeffs):
     row_count = lax.axis_size("row")
     col_count = lax.axis_size("col")
@@ -179,7 +204,7 @@
     left = lax.ppermute(left, both, turn)
     other = lax.ppermute(coeffs, both, swap)
 
-    moving = sigma.reshape(2, factor, spread, strip_rows, tile_width).transpose(2, 1, 0, 3, 4)
+    moving = strips(sigma.reshape(2, factor, spread, strip_rows, tile_width))
     moving = moving.reshape(spread * factor, 2, strip_rows, tile_width)
     moving, left = lax.optimization_barrier((moving, left))
     moving = lax.all_to_all(moving, both, 0, 0, tiled=True, axis_index_groups=plane)

time: 190 us -> 252 us (1.33)
  Pallas kernels: 12.4 us -> 77 us
  local copies, waits for them, and re-layouts: 8.36 us -> 5.23 us
    pallas_call x0 -> x1, Pallas kernels: none -> 64.7 us  [strips(): pl.pallas_call(strips_kernel, out_shape=jax.ShapeDtypeStruct((count, fact...]
    transpose x1 -> x0, local copies, waits for them, and re-layouts: 3.13 us -> none  [body(): sigma.reshape(2, factor, spread, strip_rows, tile_width)]
  transfers between devices with their start and end apart: 13 -> 13, of which waited for: 3 -> 3; matrix products, arithmetic and copies ran while one was open for 4% -> 2% of each run, Pallas kernels for 3% -> 28%
where the time goes in v4:
time: 252 us; the launch traced here: 251 us
  starting transfers between devices  89.4 us (35%)
  Pallas kernels  77 us (31%)
  blocking collectives  41.8 us (17%)
  waiting for transfers between devices  34.7 us (14%)
  local copies, waits for them, and re-layouts  5.23 us (2%)
    ppermute x8, starting transfers between devices, body(): lax.ppermute(value, both, route)  64.7 us
    pallas_call x1, Pallas kernels, strips(): pl.pallas_call(strips_kernel, out_shape=jax.ShapeDtypeStruct((count, fact...  64.7 us
    all_gather x1, blocking collectives, body(): lax.all_gather(left, 'col', axis=0, tiled=True, axis_index_groups=along_z)  41.8 us
    ppermute x8, waiting for transfers between devices, body(): lax.ppermute(value, both, route)  34.7 us
    all_to_all x1, starting transfers between devices, body(): lax.all_to_all(moving, both, 0, 0, tiled=True, axis_index_groups=plane)  9.58 us
    all_to_all x1, starting transfers between devices, body(): term = lax.all_to_all(term, 'row', 0, 0, tiled=True).sum(0)  7.25 us
    pallas_call x1, Pallas kernels, rotate(): pl.pallas_call(rotate_kernel, out_shape=jax.ShapeDtypeStruct((blocks, 2,...  6 us
  transfers between devices with their start and end apart: 13, of which 3 were waited for; matrix products, arithmetic and copies ran while one was open for 2% of the time, Pallas kernels for 28%

profile of v4, /device:TPU:6, one launch (start us, length us, event | category | flops | bytes accessed | tf_op | source)
XLA Modules:
  0.0 251.1 jit_solution(6074139052715912487)
XLA Ops:
  0.6 0.8 constant_dynamic-slice_fusion
  1.4 0.7 collective-permute-start
  2.1 64.7 %shard_map.41 = bf16[8,2,2,64,512]{4,3,2,1,0:T(8,128)(2,1)} custom-call(bf16[2,2,8,64,512]{4,3,2,1,0:T(8,128)(2,1)} %bitcast.38), custom_call_target="tpu_custom_call" | custom-call | bytes 4000000 | tf_op jit(solution)/shard_map/pallas_call | solution.py:163
  66.8 0.0 collective-permute-done
  66.8 0.0 copy-start.1
  66.8 9.6 %all-to-all-start = ((bf16[16,2,64,512]{3,2,1,0:T(8,128)(2,1)}), bf16[16,2,64,512]{3,2,1,0:T(8,128)(2,1)S(1)}, u32[]{:S(2)}, u32[]{:S(2)}) async-start(bf16[16,2,64,512]{3,2,1,0:T(8,128)(2,1)} %bitcast.40), calls=%async_computation | async-start | bytes 4194304 | tf_op jit(solution)/shard_map/all_to_all | solution.py:210
  76.4 0.0 copy-done.1
  76.4 3.4 %collective-permute-start.8 = (bf16[2,512,384]{2,1,0:T(8,128)(2,1)S(1)}, bf16[2,512,384]{2,1,0:T(8,128)(2,1)}, u32[]{:S(2)}, u32[]{:S(2)}) collective-permute-start(bf16[2,512,384]{2,1,0:T(8,128)(2,1)S(1)} %copy-done.1), channel_id=1, source_target_pairs={{0,1},{1,0},{2,3},{3,2},{4,5},{5,4},{6,7},{7,6},{8,9},{9,8},{10,11... | collective-permute-start | bytes 2359304 | tf_op jit(solution)/shard_map/ppermute | solution.py:205
  79.8 41.8 %all_gather.3 = bf16[32,32,384]{2,1,0:T(8,128)(2,1)} all-gather(bf16[2,32,384]{2,1,0:T(8,128)(2,1)S(1)} %collective-permute-done), channel_id=1, replica_groups={{0,2,4,6,8,10,12,14,16,18,20,22,24,26,28,30},{1,3,5,7,9,11,13,15,17,19,..., dimensions={0}, use_global_device_ids=true | all-gather | bytes 835584 | tf_op jit(solution)/shard_map/all_gather | solution.py:211
  121.6 0.0 all-to-all-done
  121.6 0.0 copy-start.2
  121.6 1.3 shard_map.42.near_ref
  122.9 0.0 collective-permute-done.8.other_ref
  122.9 0.0 copy-done.2
  122.9 6.0 %shard_map.43 = f32[16,2,24,384]{3,2,1,0:T(8,128)} custom-call(s32[1]{0:T(128)} %bitcast.19.which_ref, bf16[8,2,2,64,512]{4,3,2,1,0:T(8,128)(2,1)S(1)} %bitcast.35, f32[2,512,384]{2,1,0:T(8,128)S(1)} %shard_map.42.near_ref, bf16[2,512,384]{2,1,0:T(8,128)(2,1)} %collective-permute-done.8.other_ref, bf16[16,2,32,384]{3,2,1,0:T(8,128)(2,1)S(1)} %bitcast.39), custom_call_target="tpu_custom_call" | custom-call | flops 3000000000 | bytes 6000000 | tf_op jit(solution)/shard_map/pallas_call | solution.py:80
  128.9 7.2 %all-to-all-start.1 = ((f32[16,2,24,384]{3,2,1,0:T(8,128)}), f32[16,2,24,384]{3,2,1,0:T(8,128)}, u32[]{:S(2)}, u32[]{:S(2)}) async-start(f32[16,2,24,384]{3,2,1,0:T(8,128)} %shard_map.43), calls=%async_computation.1 | async-start | bytes 2359296 | tf_op jit(solution)/shard_map/all_to_all | solution.py:235
  136.1 1.2 dynamic-slice_bitcast_fusion
  137.4 3.4 %collective-permute-start.2 = (bf16[2,2,64,512]{3,2,1,0:T(8,128)(2,1)}, bf16[2,2,64,512]{3,2,1,0:T(8,128)(2,1)S(1)}, u32[]{:S(2)}, u32[]{:S(2)}) collective-permute-start(bf16[2,2,64,512]{3,2,1,0:T(8,128)(2,1)} %get-tuple-element.20), channel_id=1, source_target_pairs={{0,16},{1,17},{2,36},{3,37},{4,88},{5,89},{6,108},{7,109},{8,128},... | collective-permute-start | bytes 786440 | tf_op jit(solution)/shard_map/ppermute | solution.py:239
  140.7 6.2 %collective-permute-start.3 = (bf16[2,2,64,512]{3,2,1,0:T(8,128)(2,1)}, bf16[2,2,64,512]{3,2,1,0:T(8,128)(2,1)S(1)}, u32[]{:S(2)}, u32[]{:S(2)}) collective-permute-start(bf16[2,2,64,512]{3,2,1,0:T(8,128)(2,1)} %get-tuple-element.19), channel_id=1, source_target_pairs={{0,8},{1,9},{2,60},{3,61},{4,80},{5,81},{6,100},{7,101},{8,152},{9... | collective-permute-start | bytes 786440 | tf_op jit(solution)/shard_map/ppermute | solution.py:239
  147.0 9.9 %collective-permute-start.4 = (bf16[2,2,64,512]{3,2,1,0:T(8,128)(2,1)}, bf16[2,2,64,512]{3,2,1,0:T(8,128)(2,1)S(1)}, u32[]{:S(2)}, u32[]{:S(2)}) collective-permute-start(bf16[2,2,64,512]{3,2,1,0:T(8,128)(2,1)} %get-tuple-element.18), channel_id=1, source_target_pairs={{0,24},{1,25},{2,44},{3,45},{4,64},{5,65},{6,116},{7,117},{8,136},... | collective-permute-start | bytes 786440 | tf_op jit(solution)/shard_map/ppermute | solution.py:239
  156.9 6.6 %collective-permute-start.5 = (bf16[2,2,64,512]{3,2,1,0:T(8,128)(2,1)}, bf16[2,2,64,512]{3,2,1,0:T(8,128)(2,1)S(1)}, u32[]{:S(2)}, u32[]{:S(2)}) collective-permute-start(bf16[2,2,64,512]{3,2,1,0:T(8,128)(2,1)} %get-tuple-element.17), channel_id=1, source_target_pairs={{0,4},{1,5},{2,56},{3,57},{4,76},{5,77},{6,96},{7,97},{8,148},{9,1... | collective-permute-start | bytes 786440 | tf_op jit(solution)/shard_map/ppermute | solution.py:239
  163.5 5.6 %collective-permute-start.6 = (bf16[2,2,64,512]{3,2,1,0:T(8,128)(2,1)}, bf16[2,2,64,512]{3,2,1,0:T(8,128)(2,1)S(1)}, u32[]{:S(2)}, u32[]{:S(2)}) collective-permute-start(bf16[2,2,64,512]{3,2,1,0:T(8,128)(2,1)} %get-tuple-element.16), channel_id=1, source_target_pairs={{0,20},{1,21},{2,40},{3,41},{4,92},{5,93},{6,112},{7,113},{8,132},... | collective-permute-start | bytes 786440 | tf_op jit(solution)/shard_map/ppermute | solution.py:239
  169.0 0.7 dynamic-slice_bitcast_fusion.7
  169.8 0.0 all-to-all-done.1
  169.8 2.0 reduce_sum.18
  171.7 1.7 shard_map.44
  173.5 0.0 collective-permute-done.2.refs_1_
  173.5 4.8 %collective-permute-start.7 = (bf16[2,2,64,512]{3,2,1,0:T(8,128)(2,1)}, bf16[2,2,64,512]{3,2,1,0:T(8,128)(2,1)S(1)}, u32[]{:S(2)}, u32[]{:S(2)}) collective-permute-start(bf16[2,2,64,512]{3,2,1,0:T(8,128)(2,1)} %get-tuple-element.15), channel_id=1, source_target_pairs={{0,12},{1,13},{2,32},{3,33},{4,84},{5,85},{6,104},{7,105},{8,156},... | collective-permute-start | bytes 786440 | tf_op jit(solution)/shard_map/ppermute | solution.py:239
  178.3 13.0 %collective-permute-done.3.refs_2_ = bf16[2,2,64,512]{3,2,1,0:T(8,128)(2,1)S(1)} collective-permute-done((bf16[2,2,64,512]{3,2,1,0:T(8,128)(2,1)}, bf16[2,2,64,512]{3,2,1,0:T(8,128)(2,1)S(1)}, u32[]{:S(2)}, u32[]{:S(2)}) %collective-permute-start.3) | collective-permute-done | bytes 262176 | tf_op jit(solution)/shard_map/ppermute | solution.py:239
  191.3 1.9 collective-permute-start.1
  193.2 0.0 collective-permute-done.4.refs_3_
  193.2 26.4 %collective-permute-start.9 = (bf16[2,2,64,512]{3,2,1,0:T(8,128)(2,1)}, bf16[2,2,64,512]{3,2,1,0:T(8,128)(2,1)S(1)}, u32[]{:S(2)}, u32[]{:S(2)}) collective-permute-start(bf16[2,2,64,512]{3,2,1,0:T(8,128)(2,1)} %get-tuple-element.12), channel_id=1, source_target_pairs={{0,28},{1,29},{2,48},{3,49},{4,68},{5,69},{6,120},{7,121},{8,140},... | collective-permute-start | bytes 786440 | tf_op jit(solution)/shard_map/ppermute | solution.py:239
  219.6 3.9 %all-to-all-start.2 = ((f32[32,6,96]{2,1,0:T(8,128)}), f32[32,6,96]{2,1,0:T(8,128)S(1)}, u32[]{:S(2)}, u32[]{:S(2)}) async-start(f32[32,6,96]{2,1,0:T(8,128)} %shard_map.44), calls=%async_computation.2 | async-start | bytes 262144 | tf_op jit(solution)/shard_map/all_to_all | solution.py:240
  223.6 0.1 stack.35.place_ref
  223.7 0.0 collective-permute-done.5.refs_4_
  223.7 0.0 collective-permute-done.6.refs_5_
  223.7 9.1 %collective-permute-done.7.refs_6_ = bf16[2,2,64,512]{3,2,1,0:T(8,128)(2,1)S(1)} collective-permute-done((bf16[2,2,64,512]{3,2,1,0:T(8,128)(2,1)}, bf16[2,2,64,512]{3,2,1,0:T(8,128)(2,1)S(1)}, u32[]{:S(2)}, u32[]{:S(2)}) %collective-permute-start.7) | collective-permute-done | bytes 262176 | tf_op jit(solution)/shard_map/ppermute | solution.py:239
  232.8 0.0 collective-permute-done.1.refs_0_
  232.8 12.6 %collective-permute-done.9.refs_7_ = bf16[2,2,64,512]{3,2,1,0:T(8,128)(2,1)S(1)} collective-permute-done((bf16[2,2,64,512]{3,2,1,0:T(8,128)(2,1)}, bf16[2,2,64,512]{3,2,1,0:T(8,128)(2,1)S(1)}, u32[]{:S(2)}, u32[]{:S(2)}) %collective-permute-start.9) | collective-permute-done | bytes 262176 | tf_op jit(solution)/shard_map/ppermute | solution.py:239
  245.4 0.0 copy-start
  245.4 1.6 copy-done
  247.0 3.4 %shard_map.45 = bf16[2,1024,512]{2,1,0:T(8,128)(2,1)} custom-call(s32[8]{0:T(128)S(1)} %stack.35.place_ref, bf16[2,1024,512]{2,1,0:T(8,128)(2,1)S(1)} %copy-done, bf16[2,2,64,512]{3,2,1,0:T(8,128)(2,1)S(1)} %collective-permute-done.1.refs_0_, bf16[2,2,64,512]{3,2,1,0:T(8,128)(2,1)S(1)} %collective-permute-done.2.refs_1_, ...), custom_call_target="tpu_custom_call" | custom-call | flops 1000000000 | bytes 6000000 | tf_op jit(solution)/shard_map/pallas_call | solution.py:136
  250.3 0.0 all-to-all-done.2
  250.4 0.1 fusion
  250.5 0.7 reshape.31
  (2 shorter events, 0.0 us)
Async XLA Ops:
  1.4 65.3 %collective-permute-start = (bf16[2,32,384]{2,1,0:T(8,128)(2,1)S(1)}, bf16[2,32,384]{2,1,0:T(8,128)(2,1)S(1)}, u32[]{:S(2)}, u32[]{:S(2)}) collective-permute-start(bf16[2,32,384]{2,1,0:T(8,128)(2,1)S(1)} %constant_dynamic-slice_fusion), channel_id=1, source_target_pairs={{0,0},{1,1},{2,32},{3,33},{4,4},{5,5},{6,36},{7,37},{8,8},{9,9},{1... | collective-permute-start | bytes 147464 | tf_op jit(solution)/shard_map/ppermute | solution.py:204
  66.8 9.6 %copy-start.1 = (bf16[2,512,384]{2,1,0:T(8,128)(2,1)S(1)}, bf16[2,512,384]{2,1,0:T(8,128)(2,1)}, u32[]{:S(2)}) copy-start(bf16[2,512,384]{2,1,0:T(8,128)(2,1)} %own_ref.2) | copy-start | bytes 2359300
  66.8 54.8 %all-to-all-start = ((bf16[16,2,64,512]{3,2,1,0:T(8,128)(2,1)}), bf16[16,2,64,512]{3,2,1,0:T(8,128)(2,1)S(1)}, u32[]{:S(2)}, u32[]{:S(2)}) async-start(bf16[16,2,64,512]{3,2,1,0:T(8,128)(2,1)} %bitcast.40), calls=%async_computation | async-start | bytes 4194304 | tf_op jit(solution)/shard_map/all_to_all | solution.py:210
  76.4 46.5 %collective-permute-start.8 = (bf16[2,512,384]{2,1,0:T(8,128)(2,1)S(1)}, bf16[2,512,384]{2,1,0:T(8,128)(2,1)}, u32[]{:S(2)}, u32[]{:S(2)}) collective-permute-start(bf16[2,512,384]{2,1,0:T(8,128)(2,1)S(1)} %copy-done.1), channel_id=1, source_target_pairs={{0,1},{1,0},{2,3},{3,2},{4,5},{5,4},{6,7},{7,6},{8,9},{9,8},{10,11... | collective-permute-start | bytes 2359304 | tf_op jit(solution)/shard_map/ppermute | solution.py:205
  121.6 1.3 copy-start.2
  128.9 40.9 %all-to-all-start.1 = ((f32[16,2,24,384]{3,2,1,0:T(8,128)}), f32[16,2,24,384]{3,2,1,0:T(8,128)}, u32[]{:S(2)}, u32[]{:S(2)}) async-start(f32[16,2,24,384]{3,2,1,0:T(8,128)} %shard_map.43), calls=%async_computation.1 | async-start | bytes 2359296 | tf_op jit(solution)/shard_map/all_to_all | solution.py:235
  137.4 36.1 %collective-permute-start.2 = (bf16[2,2,64,512]{3,2,1,0:T(8,128)(2,1)}, bf16[2,2,64,512]{3,2,1,0:T(8,128)(2,1)S(1)}, u32[]{:S(2)}, u32[]{:S(2)}) collective-permute-start(bf16[2,2,64,512]{3,2,1,0:T(8,128)(2,1)} %get-tuple-element.20), channel_id=1, source_target_pairs={{0,16},{1,17},{2,36},{3,37},{4,88},{5,89},{6,108},{7,109},{8,128},... | collective-permute-start | bytes 786440 | tf_op jit(solution)/shard_map/ppermute | solution.py:239
  140.7 50.5 %collective-permute-start.3 = (bf16[2,2,64,512]{3,2,1,0:T(8,128)(2,1)}, bf16[2,2,64,512]{3,2,1,0:T(8,128)(2,1)S(1)}, u32[]{:S(2)}, u32[]{:S(2)}) collective-permute-start(bf16[2,2,64,512]{3,2,1,0:T(8,128)(2,1)} %get-tuple-element.19), channel_id=1, source_target_pairs={{0,8},{1,9},{2,60},{3,61},{4,80},{5,81},{6,100},{7,101},{8,152},{9... | collective-permute-start | bytes 786440 | tf_op jit(solution)/shard_map/ppermute | solution.py:239
  147.0 46.3 %collective-permute-start.4 = (bf16[2,2,64,512]{3,2,1,0:T(8,128)(2,1)}, bf16[2,2,64,512]{3,2,1,0:T(8,128)(2,1)S(1)}, u32[]{:S(2)}, u32[]{:S(2)}) collective-permute-start(bf16[2,2,64,512]{3,2,1,0:T(8,128)(2,1)} %get-tuple-element.18), channel_id=1, source_target_pairs={{0,24},{1,25},{2,44},{3,45},{4,64},{5,65},{6,116},{7,117},{8,136},... | collective-permute-start | bytes 786440 | tf_op jit(solution)/shard_map/ppermute | solution.py:239
  156.9 66.8 %collective-permute-start.5 = (bf16[2,2,64,512]{3,2,1,0:T(8,128)(2,1)}, bf16[2,2,64,512]{3,2,1,0:T(8,128)(2,1)S(1)}, u32[]{:S(2)}, u32[]{:S(2)}) collective-permute-start(bf16[2,2,64,512]{3,2,1,0:T(8,128)(2,1)} %get-tuple-element.17), channel_id=1, source_target_pairs={{0,4},{1,5},{2,56},{3,57},{4,76},{5,77},{6,96},{7,97},{8,148},{9,1... | collective-permute-start | bytes 786440 | tf_op jit(solution)/shard_map/ppermute | solution.py:239
  163.5 60.2 %collective-permute-start.6 = (bf16[2,2,64,512]{3,2,1,0:T(8,128)(2,1)}, bf16[2,2,64,512]{3,2,1,0:T(8,128)(2,1)S(1)}, u32[]{:S(2)}, u32[]{:S(2)}) collective-permute-start(bf16[2,2,64,512]{3,2,1,0:T(8,128)(2,1)} %get-tuple-element.16), channel_id=1, source_target_pairs={{0,20},{1,21},{2,40},{3,41},{4,92},{5,93},{6,112},{7,113},{8,132},... | collective-permute-start | bytes 786440 | tf_op jit(solution)/shard_map/ppermute | solution.py:239
  173.5 59.3 %collective-permute-start.7 = (bf16[2,2,64,512]{3,2,1,0:T(8,128)(2,1)}, bf16[2,2,64,512]{3,2,1,0:T(8,128)(2,1)S(1)}, u32[]{:S(2)}, u32[]{:S(2)}) collective-permute-start(bf16[2,2,64,512]{3,2,1,0:T(8,128)(2,1)} %get-tuple-element.15), channel_id=1, source_target_pairs={{0,12},{1,13},{2,32},{3,33},{4,84},{5,85},{6,104},{7,105},{8,156},... | collective-permute-start | bytes 786440 | tf_op jit(solution)/shard_map/ppermute | solution.py:239
  191.3 41.5 %collective-permute-start.1 = (bf16[2,2,64,512]{3,2,1,0:T(8,128)(2,1)}, bf16[2,2,64,512]{3,2,1,0:T(8,128)(2,1)S(1)}, u32[]{:S(2)}, u32[]{:S(2)}) collective-permute-start(bf16[2,2,64,512]{3,2,1,0:T(8,128)(2,1)} %dynamic-slice_bitcast_fusion.7), channel_id=1, source_target_pairs={{0,0},{1,1},{2,52},{3,53},{4,72},{5,73},{6,124},{7,125},{8,144},{9... | collective-permute-start | bytes 786440 | tf_op jit(solution)/shard_map/ppermute | solution.py:239
  193.2 52.2 %collective-permute-start.9 = (bf16[2,2,64,512]{3,2,1,0:T(8,128)(2,1)}, bf16[2,2,64,512]{3,2,1,0:T(8,128)(2,1)S(1)}, u32[]{:S(2)}, u32[]{:S(2)}) collective-permute-start(bf16[2,2,64,512]{3,2,1,0:T(8,128)(2,1)} %get-tuple-element.12), channel_id=1, source_target_pairs={{0,28},{1,29},{2,48},{3,49},{4,68},{5,69},{6,120},{7,121},{8,140},... | collective-permute-start | bytes 786440 | tf_op jit(solution)/shard_map/ppermute | solution.py:239
  219.6 30.7 %all-to-all-start.2 = ((f32[32,6,96]{2,1,0:T(8,128)}), f32[32,6,96]{2,1,0:T(8,128)S(1)}, u32[]{:S(2)}, u32[]{:S(2)}) async-start(f32[32,6,96]{2,1,0:T(8,128)} %shard_map.44), calls=%async_computation.2 | async-start | bytes 262144 | tf_op jit(solution)/shard_map/all_to_all | solution.py:240
  245.4 1.6 copy-start
